TPU v7x, 32 devices: a whole 2x2x4 slice. The times are simulated.
32 devices in a mesh: dp: 8 (over y, x, core), tensor: 4 (over z).
Axes of the slice: x: 2, y: 2, z: 4, core: 2. Of those that a mesh axis runs over, the one named last changes fastest.
Arguments:
- activations: bfloat16 [8192, 5120], P('dp', 'tensor'), may hold values from -36 to 36, as said below
- out_grads: bfloat16 [8192, 4096], P('dp', 'tensor'), may hold values from -0.04375 to 0.04375, as said below
Outputs:
- combined: float32 [5120, 4096], P('dp', 'tensor')
Inputs may be any that keep to these rules, and one draw needn't show every extreme that they name: Replicas' activations share a common part and features have different scales. `out_grads`: Replicas' output gradients share a common part and columns have different scales.
All inputs are finite; a program needn't handle non-finite values.
Results may differ from a plain program's by a relative error of at most 0.0003.
Values may be sent and summed in bfloat16 or wider, within the bound.
A program may use at most 128 MiB of HBM per device.

v0:
```python
import jax
import jax.numpy as jnp
from jax import lax
from jax.sharding import PartitionSpec as P

epsilon = 1e-06


def swapped(x, axis, apart):
    return lax.ppermute(x, axis, [(i, i ^ 1 << apart) for i in range(lax.axis_size(axis))])


def group_totals(partials, section):
    for bit_number in range(section + 1):
        partials = partials + swapped(partials, "dp", bit_number)
    return lax.psum(partials, "tensor")


def adasum_pair(mine, other, section, replica):
    upper_side = jnp.right_shift(replica, section) % 2 == 1
    mine_norm = jnp.sum(mine * mine)
    other_norm = jnp.sum(other * other)
    lower_norm = jnp.where(upper_side, other_norm, mine_norm)
    upper_norm = jnp.where(upper_side, mine_norm, other_norm)
    partials = jnp.stack([jnp.sum(mine * other), lower_norm, upper_norm])
    totals = group_totals(partials, section)
    lower_coef = 1.0 - totals[0] / (2.0 * (totals[1] + epsilon))
    upper_coef = 1.0 - totals[0] / (2.0 * (totals[2] + epsilon))
    mine_coef = jnp.where(upper_side, upper_coef, lower_coef)
    other_coef = jnp.where(upper_side, lower_coef, upper_coef)
    return mine_coef * mine + other_coef * other


def on_device(activations, out_grads):
    replicas = lax.axis_size("dp")
    section_count = replicas.bit_length() - 1
    replica = lax.axis_index("dp")
    columns = out_grads.shape[1]
    slab_rows = activations.shape[1]
    block_rows = slab_rows * lax.axis_size("tensor") // replicas
    full_grad = jnp.einsum(
        "tk,tf->kf",
        lax.all_gather(activations, "tensor", axis=1, tiled=True),
        out_grads,
        preferred_element_type=jnp.float32,
    )
    holding = full_grad.reshape(replicas, block_rows, columns)
    start_section = 0
    for section in range(start_section, section_count):
        section_bit = jnp.right_shift(replica, section) % 2
        paired = holding.reshape(-1, 2, block_rows, columns)
        keeping = lax.dynamic_index_in_dim(paired, section_bit, axis=1, keepdims=False)
        sending = lax.dynamic_index_in_dim(paired, 1 - section_bit, axis=1, keepdims=False)
        received = swapped(sending, "dp", section)
        holding = adasum_pair(keeping, received, section, replica)
    return holding.reshape(block_rows, columns)


def solution(mesh):
    return jax.shard_map(
        on_device,
        mesh=mesh,
        in_specs=(P("dp", "tensor"), P("dp", "tensor")),
        out_specs=P("dp", "tensor"),
        check_vma=False,
    )
```

profile of v0, /device:TPU:0, one launch (start us, length us, event | category | flops | bytes accessed | tf_op | source)
XLA Modules:
  0.0 534.6 jit_solution(741606797234651110)
XLA Ops:
  7.3 188.3 %all-gather.2.cloned.1.call-done = bf16[1024,5120]{1,0:T(8,128)(2,1)} async-done(((bf16[1024,1280]{1,0:T(8,128)(2,1)}), bf16[1024,5120]{1,0:T(8,128)(2,1)}) %all-gather.2.cloned.1.call-update) | async-done | bytes 10485776 | tf_op jit(solution)/shard_map/all_gather | solution.py:43
  195.6 17.6 %fusion.9 = f32[5120,1024]{1,0:T(8,128)} fusion(bf16[1024,5120]{1,0:T(8,128)(2,1)} %all-gather.2.cloned.1.call-done, bf16[1024,1024]{1,0:T(8,128)(2,1)S(1)} %copy-done), kind=kOutput, calls=%fused_computation.27 | convolution fusion | flops 10737418240 | bytes 33554432 | tf_op jit(solution)/shard_map/tk,tf->kf/dot_general | solution.py:41
  213.2 10.1 %dynamic-slice_bitcast_fusion = f32[4,640,1024]{2,1,0:T(8,128)} fusion(f32[4,2,640,1024]{3,2,1,0:T(8,128)} %bitcast.48, s32[]{:T(128)S(6)} %select_n.83), kind=kLoop, calls=%fused_computation.7 | loop fusion | bytes 20971524 | tf_op jit(solution)/shard_map/jit(dynamic_index_in_dim)/squeeze | solution.py:53
  223.4 16.4 %collective-permute-done = f32[4,640,1024]{2,1,0:T(8,128)} collective-permute-done((f32[4,640,1024]{2,1,0:T(8,128)}, f32[4,640,1024]{2,1,0:T(8,128)}, u32[]{:S(2)}, u32[]{:S(2)}) %collective-permute-start) | collective-permute-done | bytes 10485792 | tf_op jit(solution)/shard_map/ppermute | solution.py:10
  239.9 8.8 %fusion = (f32[]{:T(128)}, f32[]{:T(128)}, f32[]{:T(128)}) fusion(f32[4,640,1024]{2,1,0:T(8,128)} %collective-permute-done, f32[4,2,640,1024]{3,2,1,0:T(8,128)} %bitcast.49, s32[]{:T(128)S(6)} %select_n.82), kind=kLoop, calls=%fused_computation.3 | loop fusion | flops 15728637 | bytes 20971536 | tf_op jit(solution)/shard_map/reduce_sum | solution.py:25
  251.2 0.7 pad_maximum_fusion
  252.1 0.9 collective-permute-done.1
  253.7 8.8 %psum.21 = f32[3]{0:T(128)S(1)} all-reduce(f32[3]{0:T(128)S(1)} %fusion.14), channel_id=1, replica_groups=mesh['dp'=8,'tensor'=4] {'tensor'}, use_global_device_ids=true, to_apply=%region_3.4 | all-reduce | flops 3 | bytes 24 | tf_op jit(solution)/shard_map/psum | solution.py:16
  265.6 14.9 %fusion.2 = f32[4,640,1024]{2,1,0:T(8,128)} fusion(f32[4,640,1024]{2,1,0:T(8,128)} %collective-permute-done, f32[4,2,640,1024]{3,2,1,0:T(8,128)} %bitcast.50, s32[]{:T(128)S(6)} %select_n.82, f32[]{:T(128)S(6)} %select_n.87, f32[]{:T(128)S(6)} %select_n.86), kind=kLoop, calls=%fused_computation.5 | loop fusion | flops 7864320 | bytes 31457292 | tf_op jit(solution)/shard_map/add | solution.py:31
  280.5 5.7 %dynamic-slice_bitcast_fusion.1 = f32[2,640,1024]{2,1,0:T(8,128)} fusion(f32[2,2,640,1024]{3,2,1,0:T(8,128)} %bitcast.45, s32[]{:T(128)S(6)} %select_n.89), kind=kLoop, calls=%fused_computation.15 | loop fusion | bytes 10485764 | tf_op jit(solution)/shard_map/jit(dynamic_index_in_dim)/squeeze | solution.py:53
  286.2 1.7 collective-permute-start.2
  287.9 111.8 %collective-permute-done.2 = f32[2,640,1024]{2,1,0:T(8,128)} collective-permute-done((f32[2,640,1024]{2,1,0:T(8,128)}, f32[2,640,1024]{2,1,0:T(8,128)}, u32[]{:S(2)}, u32[]{:S(2)}) %collective-permute-start.2) | collective-permute-done | bytes 5242912 | tf_op jit(solution)/shard_map/ppermute | solution.py:10
  399.7 6.1 %fusion.3 = (f32[]{:T(128)}, f32[]{:T(128)}, f32[]{:T(128)}) fusion(f32[2,640,1024]{2,1,0:T(8,128)} %collective-permute-done.2, f32[2,2,640,1024]{3,2,1,0:T(8,128)} %bitcast.46, s32[]{:T(128)S(6)} %select_n.88), kind=kLoop, calls=%fused_computation.11 | loop fusion | flops 7864317 | bytes 10485776 | tf_op jit(solution)/shard_map/reduce_sum | solution.py:25
  408.3 0.7 pad_maximum_fusion.1
  409.0 1.1 collective-permute-done.3
  410.9 1.7 collective-permute-start.4
  412.5 1.9 collective-permute-done.4
  415.1 10.2 %psum.22 = f32[3]{0:T(128)S(1)} all-reduce(f32[3]{0:T(128)S(1)} %fusion.16), channel_id=1, replica_groups=mesh['dp'=8,'tensor'=4] {'tensor'}, use_global_device_ids=true, to_apply=%region_7.8 | all-reduce | flops 3 | bytes 24 | tf_op jit(solution)/shard_map/psum | solution.py:16
  428.5 5.3 fusion.5
  433.9 2.3 copy-done.2
  436.2 1.7 constant_dynamic-slice_fusion
  437.8 1.5 collective-permute-start.5
  439.3 54.6 %collective-permute-done.5 = f32[1,640,1024]{2,1,0:T(8,128)} collective-permute-done((f32[1,640,1024]{2,1,0:T(8,128)}, f32[1,640,1024]{2,1,0:T(8,128)}, u32[]{:S(2)}, u32[]{:S(2)}) %collective-permute-start.5) | collective-permute-done | bytes 2621472 | tf_op jit(solution)/shard_map/ppermute | solution.py:10
  494.0 4.0 multiply_reduce_fusion.4
  500.5 0.7 pad_maximum_fusion.2
  501.2 1.1 collective-permute-done.6
  503.1 1.5 collective-permute-start.7
  504.6 2.0 collective-permute-done.7
  507.3 1.5 collective-permute-start.8
  508.8 2.0 collective-permute-done.8
  510.9 8.7 %psum.23 = f32[3]{0:T(128)S(1)} all-reduce(f32[3]{0:T(128)S(1)} %add.114), channel_id=1, replica_groups=mesh['dp'=8,'tensor'=4] {'tensor'}, use_global_device_ids=true, to_apply=%region_11.12 | all-reduce | flops 3 | bytes 24 | tf_op jit(solution)/shard_map/psum | solution.py:16
  522.8 4.9 add_bitcast_fusion
  (20 shorter events, 6.5 us)
Async XLA Ops:
  6.5 189.1 %copy-start = (bf16[1024,1024]{1,0:T(8,128)(2,1)S(1)}, bf16[1024,1024]{1,0:T(8,128)(2,1)}, u32[]{:S(2)}) copy-start(bf16[1024,1024]{1,0:T(8,128)(2,1)} %param.3) | copy-start | bytes 6291460
  6.5 189.0 %all-gather.2.cloned.1.call-start = ((), (), s32[]{:S(2)}) async-start(), calls=%async_computation | async-start | bytes 13107200 | tf_op jit(solution)/shard_map/all_gather | solution.py:43
  223.4 16.5 %collective-permute-start = (f32[4,640,1024]{2,1,0:T(8,128)}, f32[4,640,1024]{2,1,0:T(8,128)}, u32[]{:S(2)}, u32[]{:S(2)}) collective-permute-start(f32[4,640,1024]{2,1,0:T(8,128)} %dynamic-slice_bitcast_fusion), channel_id=1, source_target_pairs={{0,4},{4,0},{8,12},{12,8},{16,20},{20,16},{24,28},{28,24},{1,5},{5... | collective-permute-start | bytes 31457288 | tf_op jit(solution)/shard_map/ppermute | solution.py:10
  251.9 1.1 collective-permute-start.1
  286.2 113.5 %collective-permute-start.2 = (f32[2,640,1024]{2,1,0:T(8,128)}, f32[2,640,1024]{2,1,0:T(8,128)}, u32[]{:S(2)}, u32[]{:S(2)}) collective-permute-start(f32[2,640,1024]{2,1,0:T(8,128)} %dynamic-slice_bitcast_fusion.1), channel_id=1, source_target_pairs={{0,8},{4,12},{8,0},{12,4},{16,24},{20,28},{24,16},{28,20},{1,9},{5... | collective-permute-start | bytes 15728648 | tf_op jit(solution)/shard_map/ppermute | solution.py:10
  409.0 1.1 collective-permute-start.3
  410.9 3.5 collective-permute-start.4
  433.9 2.3 copy-start.2
  437.8 56.1 %collective-permute-start.5 = (f32[1,640,1024]{2,1,0:T(8,128)}, f32[1,640,1024]{2,1,0:T(8,128)}, u32[]{:S(2)}, u32[]{:S(2)}) collective-permute-start(f32[1,640,1024]{2,1,0:T(8,128)} %constant_dynamic-slice_fusion), channel_id=1, source_target_pairs={{0,16},{4,20},{8,24},{12,28},{16,0},{20,4},{24,8},{28,12},{1,17},{... | collective-permute-start | bytes 7864328 | tf_op jit(solution)/shard_map/ppermute | solution.py:10
  494.0 33.8 %copy-start.1 = (bf16[1024,1024]{1,0:T(8,128)(2,1)S(1)}, bf16[1024,1024]{1,0:T(8,128)(2,1)}, u32[]{:S(2)}) copy-start(bf16[1024,1024]{1,0:T(8,128)(2,1)} %param.3) | copy-start | bytes 6291460
  501.2 1.1 collective-permute-start.6
  503.1 3.5 collective-permute-start.7
  507.3 3.5 collective-permute-start.8
Sparse Core Ops, SparseCore 0:
  8.9 186.6 all-gather.1
where the time goes:
time: 535 us
  waiting for transfers between devices  381 us (71%)
  other arithmetic  49.8 us (9%)
  between operations  28.6 us (5%)
  blocking collectives  27.7 us (5%)
  local copies, waits for them, and re-layouts  21.7 us (4%)
  matrix products  17.6 us (3%)
  starting transfers between devices  8.17 us (2%)
    ppermute x9, waiting for transfers between devices, swapped(): lax.ppermute(x, axis, [(i, i ^ 1 << apart) for i in range(lax.axis_size(a...  192 us
    all_gather x1, waiting for transfers between devices, on_device(): lax.all_gather(activations, 'tensor', axis=1, tiled=True)  188 us
    psum x3, blocking collectives, group_totals(): return lax.psum(partials, 'tensor')  27.7 us
    add x2, other arithmetic, adasum_pair(): return mine_coef * mine + other_coef * other  20.2 us
    reduce_sum x3, other arithmetic, adasum_pair(): partials = jnp.stack([jnp.sum(mine * other), lower_norm, upper_norm])  18.9 us
    dot_general x1, matrix products, on_device(): jnp.einsum('tk,tf->kf', lax.all_gather(activations, 'tensor', axis=1, til...  17.6 us
    squeeze x3, local copies, waits for them, and re-layouts, on_device(): lax.dynamic_index_in_dim(paired, 1 - section_bit, axis=1, keepdims=False)  17.5 us
  transfers between devices with their start and end apart: 10, of which 10 were waited for; matrix products, arithmetic and copies ran while one was open for 0% of the time, Pallas kernels for 0%

commit v1 on v0

--- a/solution.py
+++ b/solution.py
@@ -1,9 +1,14 @@
+import functools
 import jax
 import jax.numpy as jnp
 from jax import lax
+from jax.experimental import pallas as pl
+from jax.experimental.pallas import tpu as pltpu
 from jax.sharding import PartitionSpec as P
 
 epsilon = 1e-06
+MESH = pl.DeviceIdType.MESH
+CHUNKS = 4
 
 
 def swapped(x, axis, apart):
@@ -31,7 +36,7 @@
     return mine_coef * mine + other_coef * other
 
 
-def on_device(activations, out_grads):
+def by_halving(activations, out_grads):
     replicas = lax.axis_size("dp")
     section_count = replicas.bit_length() - 1
     replica = lax.axis_index("dp")
@@ -45,8 +50,7 @@
         preferred_element_type=jnp.float32,
     )
     holding = full_grad.reshape(replicas, block_rows, columns)
-    start_section = 0
-    for section in range(start_section, section_count):
+    for section in range(section_count):
         section_bit = jnp.right_shift(replica, section) % 2
         paired = holding.reshape(-1, 2, block_rows, columns)
         keeping = lax.dynamic_index_in_dim(paired, section_bit, axis=1, keepdims=False)
@@ -56,7 +60,324 @@
     return holding.reshape(block_rows, columns)
 
 
+def pair_list(count):
+    return [(a, b) for a in range(count) for b in range(a, count)]
+
+
+def tree_weights(gram, count):
+    weights = [[(r, None)] for r in range(count)]
+    while count > 1:
+        half = count // 2
+        low, high = [], []
+        for i in range(half):
+            aa, bb, ab = gram[2 * i, 2 * i], gram[2 * i + 1, 2 * i + 1], gram[2 * i, 2 * i + 1]
+            bound = jnp.sqrt(aa) * jnp.sqrt(bb)
+            ab = jnp.clip(ab, -bound, bound)
+            low.append(1.0 - ab / (2.0 * (aa + epsilon)))
+            high.append(1.0 - ab / (2.0 * (bb + epsilon)))
+        merged = {}
+        for i, j in pair_list(half):
+            cross = gram[2 * i, 2 * j + 1]
+            back = gram[2 * i + 1, 2 * j] if i != j else cross
+            value = (
+                low[i] * (low[j] * gram[2 * i, 2 * j] + high[j] * cross)
+                + high[i] * (low[j] * back + high[j] * gram[2 * i + 1, 2 * j + 1])
+            )
+            merged[i, j] = jnp.maximum(value, 0.0) if i == j else value
+        weights = [
+            [(r, low[i] if w is None else w * low[i]) for r, w in weights[2 * i]]
+            + [(r, high[i] if w is None else w * high[i]) for r, w in weights[2 * i + 1]]
+            for i in range(half)
+        ]
+        gram, count = merged, half
+    return [w for _, w in sorted(weights[0], key=lambda item: item[0])]
+
+
+def kernel(
+    R, Z, x_ref, y_ref, out_ref, fw,
+    xg, yg, grads, part, first, second,
+    zsend, zrecv, xsend, xrecv, ysend, yrecv, fsend, lsem, asend, arecv, bsend, brecv,
+):
+    me = lax.axis_index("dp")
+    z = lax.axis_index("tensor")
+    chips = R // 2
+    chip, core = me // 2, me % 2
+    sibling = chip * 2 + 1 - core
+    rows = x_ref.shape[0] // CHUNKS
+    width = xg.shape[2]
+    columns = yg.shape[2]
+
+    barrier = pltpu.get_barrier_semaphore()
+    for j in range(1, Z):
+        pl.semaphore_signal(barrier, inc=1, device_id=(me, (z + j) % Z), device_id_type=MESH)
+    for j in range(1, R):
+        pl.semaphore_signal(barrier, inc=1, device_id=((me + j) % R, z), device_id_type=MESH)
+    pl.semaphore_wait(barrier, Z + R - 2)
+
+    def remote(src, dst, send, recv, device):
+        return pltpu.make_async_remote_copy(
+            src_ref=src, dst_ref=dst, send_sem=send, recv_sem=recv,
+            device_id=device, device_id_type=MESH,
+        )
+
+    def span(i):
+        return pl.ds(pl.multiple_of(i * rows, rows), rows)
+
+    def z_copy(src, s, i, way):
+        to = z + 1 if way == 0 else z - 1
+        return remote(
+            src, fw.at[s, span(i)], zsend.at[way, s, i], zrecv.at[s, i], (me, to)
+        )
+
+    def own(i):
+        return x_ref.at[span(i)]
+
+    def held(s, i):
+        return fw.at[s, span(i)]
+
+    def scatter(src, s, i, start):
+        for h in range(2):
+            dest = 2 * s + h
+            piece = src.at[:, pl.ds(h * width, width)]
+
+            @pl.when(dest == me)
+            def _():
+                if start:
+                    pltpu.make_async_copy(piece, xg.at[me, span(i)], xrecv.at[me, i]).start()
+
+            @pl.when(dest != me)
+            def _():
+                copy = remote(
+                    piece, xg.at[me, span(i)], xsend.at[s, i, h], xrecv.at[me, i], (dest, z)
+                )
+                if start:
+                    copy.start()
+                else:
+                    copy.wait_send()
+
+    def move_along(start):
+        @pl.loop(0, CHUNKS)
+        def _(i):
+            for way, there in ((0, z < Z - 1), (1, z > 0)):
+                @pl.when(there)
+                def _():
+                    copy = z_copy(own(i), z, i, way)
+                    if start:
+                        copy.start()
+                    else:
+                        copy.wait_send()
+            scatter(own(i), z, i, start)
+
+        if start:
+            send_out_grads()
+
+        for t in range(1, Z):
+            @pl.loop(0, CHUNKS)
+            def _(i):
+                for way, s, exists, further in (
+                    (0, z - t, z - t >= 0, z < Z - 1),
+                    (1, z + t, z + t < Z, z > 0),
+                ):
+                    @pl.when(exists)
+                    def _():
+                        if start:
+                            z_copy(held(s, i), s, i, way).wait_recv()
+
+                        @pl.when(further)
+                        def _():
+                            copy = z_copy(held(s, i), s, i, way)
+                            if start:
+                                copy.start()
+                            else:
+                                copy.wait_send()
+                        scatter(held(s, i), s, i, start)
+
+            if start and t == Z - 2:
+                share_out_grads()
+
+    def y_copy(j):
+        return remote(
+            y_ref, yg.at[me], ysend.at[j], yrecv.at[me], (((chip + j) % chips) * 2 + core, z)
+        )
+
+    def sibling_copy():
+        return remote(y_ref, yg.at[me], ysend.at[0], yrecv.at[me], (sibling, z))
+
+    def share_copy(j):
+        r = ((chip + j) % chips) * 2 + core
+        return remote(yg.at[r], yg.at[r], fsend.at[j], yrecv.at[r], (sibling, z))
+
+    def local_y():
+        return pltpu.make_async_copy(y_ref, yg.at[me], lsem)
+
+    def send_out_grads():
+        for j in range(1, chips):
+            y_copy(j).start()
+        sibling_copy().start()
+        local_y().start()
+
+    def share_out_grads():
+        for j in range(1, chips):
+            r = ((chip + j) % chips) * 2 + core
+            remote(yg.at[r], yg.at[r], fsend.at[j], yrecv.at[r], (sibling, z)).wait_recv()
+            share_copy(j).start()
+
+    move_along(True)
+
+    local_y().wait()
+    for j in range(chips):
+        r = ((chip + j) % chips) * 2 + 1 - core
+        remote(yg.at[r], yg.at[r], fsend.at[j], yrecv.at[r], (sibling, z)).wait_recv()
+
+    tile = 256
+
+    @pl.loop(0, CHUNKS)
+    def _(i):
+        @pl.loop(0, R)
+        def _(r):
+            pltpu.make_async_copy(xg.at[r, span(i)], xg.at[r, span(i)], xrecv.at[r, i]).wait()
+
+            @pl.loop(0, columns // tile)
+            def _(q):
+                at = pl.ds(pl.multiple_of(q * tile, tile), tile)
+                product = lax.dot_general(
+                    xg[r, span(i), :], yg[r, span(i), at], (((0,), (0,)), ((), ())),
+                    preferred_element_type=jnp.float32,
+                )
+
+                @pl.when(i == 0)
+                def _():
+                    grads[r, :, at] = product
+
+                @pl.when(i > 0)
+                def _():
+                    grads[r, :, at] += product
+
+    pairs = pair_list(R)
+
+    def accumulate(b, sums):
+        at = pl.ds(pl.multiple_of(b * 8, 8), 8)
+        sums = list(sums)
+        for q in range(columns // 128):
+            blocks = [grads[r, at, pl.ds(q * 128, 128)] for r in range(R)]
+            for n, (a, c) in enumerate(pairs):
+                sums[n] = sums[n] + blocks[a] * blocks[c]
+        return tuple(sums)
+
+    sums = lax.fori_loop(
+        0, width // 8, accumulate, tuple(jnp.zeros((8, 128), jnp.float32) for _ in pairs)
+    )
+    part[0] = jnp.zeros(part.shape[1:], jnp.float32)
+    for n in range(len(pairs)):
+        part[0, pl.ds(n, 1), :] = jnp.sum(sums[n], axis=0, keepdims=True)
+
+    def around_z(j):
+        return remote(part.at[0], first.at[j - 1], asend.at[j - 1], arecv.at[j - 1], (me, (z + j) % Z))
+
+    def around_plane(j):
+        return remote(
+            part.at[1], second.at[j - 1], bsend.at[j - 1], brecv.at[j - 1], ((me + j) % R, z)
+        )
+
+    for j in range(1, Z):
+        around_z(j).start()
+    for j in range(1, Z):
+        around_z(j).wait_recv()
+    part[1] = part[0] + sum(first[j - 1] for j in range(1, Z))
+    for j in range(1, R):
+        around_plane(j).start()
+    for j in range(1, R):
+        around_plane(j).wait_recv()
+    totals = part[1] + sum(second[j - 1] for j in range(1, R))
+    totals = jnp.sum(totals, axis=1, keepdims=True)
+    gram = {pair: totals[n:n + 1, :] for n, pair in enumerate(pairs)}
+    weights = tree_weights(gram, R)
+
+    band = 16
+
+    @pl.loop(0, width // band)
+    def _(b):
+        at = pl.ds(pl.multiple_of(b * band, band), band)
+        total = weights[0] * grads[0, at, :]
+        for r in range(1, R):
+            total = total + weights[r] * grads[r, at, :]
+        out_ref[at, :] = total
+
+    move_along(False)
+    for j in range(1, chips):
+        y_copy(j).wait_send()
+        share_copy(j).wait_send()
+    sibling_copy().wait_send()
+    for j in range(1, Z):
+        around_z(j).wait_send()
+    for j in range(1, R):
+        around_plane(j).wait_send()
+
+
+def by_tiles(R, Z, activations, out_grads):
+    tokens, slab = activations.shape
+    columns = out_grads.shape[1]
+    width = slab * Z // R
+    kept = -(-len(pair_list(R)) // 8) * 8
+    dma = pltpu.SemaphoreType.DMA
+    return pl.pallas_call(
+        functools.partial(kernel, R, Z),
+        out_shape=(
+            jax.ShapeDtypeStruct((width, columns), jnp.float32),
+            jax.ShapeDtypeStruct((Z, tokens, slab), jnp.bfloat16),
+        ),
+        in_specs=[pl.BlockSpec(memory_space=pl.ANY)] * 2,
+        out_specs=(
+            pl.BlockSpec(memory_space=pltpu.VMEM),
+            pl.BlockSpec(memory_space=pl.ANY),
+        ),
+        scratch_shapes=[
+            pltpu.VMEM((R, tokens, width), jnp.bfloat16),
+            pltpu.VMEM((R, tokens, columns), jnp.bfloat16),
+            pltpu.VMEM((R, width, columns), jnp.float32),
+            pltpu.VMEM((2, kept, 128), jnp.float32),
+            pltpu.VMEM((Z - 1, kept, 128), jnp.float32),
+            pltpu.VMEM((R - 1, kept, 128), jnp.float32),
+            dma((2, Z, CHUNKS)),
+            dma((Z, CHUNKS)),
+            dma((Z, CHUNKS, 2)),
+            dma((R, CHUNKS)),
+            dma((R // 2,)),
+            dma((R,)),
+            dma((R // 2,)),
+            dma,
+            dma((Z - 1,)),
+            dma((Z - 1,)),
+            dma((R - 1,)),
+            dma((R - 1,)),
+        ],
+        compiler_params=pltpu.CompilerParams(
+            collective_id=0, has_side_effects=True, vmem_limit_bytes=60 * 1024 * 1024
+        ),
+        cost_estimate=pl.CostEstimate(
+            flops=2 * R * tokens * width * columns,
+            bytes_accessed=2 * R * tokens * (width + columns),
+            transcendentals=0,
+        ),
+    )(activations, out_grads)[0]
+
+
 def solution(mesh):
+    R, Z = mesh.shape["dp"], mesh.shape["tensor"]
+
+    def on_device(activations, out_grads):
+        tokens, slab = activations.shape
+        columns = out_grads.shape[1]
+        width = slab * Z // R
+        fits = (
+            R == 2 * Z and R <= 8 and width % 128 == 0 and columns % 256 == 0
+            and tokens % (CHUNKS * 16) == 0
+            and R * (2 * tokens * (width + columns) + 4 * width * columns) < 50 * 2**20
+        )
+        if fits:
+            return by_tiles(R, Z, activations, out_grads)
+        return by_halving(activations, out_grads)
+
     return jax.shard_map(
         on_device,
         mesh=mesh,

time: 535 us -> 300 us (0.56)
  waiting for transfers between devices: 381 us -> 0 us
  Pallas kernels: 0 us -> 296 us
  other arithmetic: 49.8 us -> 0 us
  between operations: 28.6 us -> 0.01 us
  blocking collectives: 27.7 us -> 0 us
  local copies, waits for them, and re-layouts: 21.7 us -> 3.56 us
  matrix products: 17.6 us -> 0 us
  starting transfers between devices: 8.17 us -> 0 us
    pallas_call x0 -> x1, Pallas kernels: none -> 296 us  [by_tiles(): pl.pallas_call(functools.partial(kernel, R, Z), out_shape=(jax.ShapeDtype...]
    ppermute x9 -> x0, waiting for transfers between devices: 192 us -> none  [swapped(): lax.ppermute(x, axis, [(i, i ^ 1 << apart) for i in range(lax.axis_size(a...]
    all_gather x1 -> x0, waiting for transfers between devices: 188 us -> none  [on_device(): lax.all_gather(activations, 'tensor', axis=1, tiled=True)]
    psum x3 -> x0, blocking collectives: 27.7 us -> none  [group_totals(): return lax.psum(partials, 'tensor')]
    add x8 -> x0, other arithmetic: 23.8 us -> none  [the longest x2 20.2 us: adasum_pair(): return mine_coef * mine + other_coef * other]
    reduce_sum x3 -> x0, other arithmetic: 18.9 us -> none  [adasum_pair(): partials = jnp.stack([jnp.sum(mine * other), lower_norm, upper_norm])]
    dot_general x1 -> x0, matrix products: 17.6 us -> none  [on_device(): jnp.einsum('tk,tf->kf', lax.all_gather(activations, 'tensor', axis=1, til...]
    squeeze x3 -> x0, local copies, waits for them, and re-layouts: 17.5 us -> none  [on_device(): lax.dynamic_index_in_dim(paired, 1 - section_bit, axis=1, keepdims=False)]
  transfers between devices with their start and end apart: 10 -> 0, of which waited for: 10 -> 0; matrix products, arithmetic and copies ran while one was open for 0% -> 0% of each run, Pallas kernels for 0% -> 0%
where the time goes in v1:
time: 300 us
  Pallas kernels  296 us (99%)
  local copies, waits for them, and re-layouts  3.56 us (1%)
    pallas_call x1, Pallas kernels, by_tiles(): pl.pallas_call(functools.partial(kernel, R, Z), out_shape=(jax.ShapeDtype...  296 us

profile of v1, /device:TPU:0, one launch (start us, length us, event | category | flops | bytes accessed | tf_op | source)
XLA Modules:
  0.0 299.5 jit_solution(1605835443270136372)
XLA Ops:
  0.0 296.0 %shard_map.28 = (f32[640,1024]{1,0:T(8,128)}, bf16[4,1024,1280]{2,1,0:T(8,128)(2,1)}) custom-call(bf16[1024,1280]{1,0:T(8,128)(2,1)} %x_ref.1, bf16[1024,1024]{1,0:T(8,128)(2,1)} %y_ref.1), custom_call_target="tpu_custom_call" | custom-call | flops 10737418240 | bytes 27262976 | tf_op jit(solution)/shard_map/pallas_call | solution.py:323
  296.0 3.6 %copy.4 = f32[640,1024]{1,0:T(8,128)} copy(f32[640,1024]{1,0:T(8,128)} %get-tuple-element.6) | data formatting | bytes 5242880

commit v2 on v1

--- a/solution.py
+++ b/solution.py
@@ -8,7 +8,8 @@
 
 epsilon = 1e-06
 MESH = pl.DeviceIdType.MESH
-CHUNKS = 4
+CHUNKS = 8
+FOLD = 2
 
 
 def swapped(x, axis, apart):
@@ -96,16 +97,27 @@
 def kernel(
     R, Z, x_ref, y_ref, out_ref, fw,
     xg, yg, grads, part, first, second,
-    zsend, zrecv, xsend, xrecv, ysend, yrecv, fsend, lsem, asend, arecv, bsend, brecv,
+    esend, zrecv, xsend, xrecv, rsend, lsend, ysend, yrecv, psend, fsend, lsem,
+    asend, arecv, bsend, brecv,
 ):
     me = lax.axis_index("dp")
     z = lax.axis_index("tensor")
     chips = R // 2
+    last = chips - 1
     chip, core = me // 2, me % 2
     sibling = chip * 2 + 1 - core
     rows = x_ref.shape[0] // CHUNKS
     width = xg.shape[2]
     columns = yg.shape[2]
+
+    def across(c, way):
+        return (c // 2) * 2 + 1 - c % 2 if way == 0 else (1 - c // 2) * 2 + c % 2
+
+    side, above = across(chip, 0), across(chip, 1)
+    opposite = across(side, 1)
+    order = (chip, side, above, opposite)
+    via = jnp.where(core == 0, side, above)
+    other = jnp.where(core == 0, above, side)
 
     barrier = pltpu.get_barrier_semaphore()
     for j in range(1, Z):
@@ -120,138 +132,229 @@
             device_id=device, device_id_type=MESH,
         )
 
+    def go(copy, start):
+        if start:
+            copy.start()
+        else:
+            copy.wait_send()
+
     def span(i):
         return pl.ds(pl.multiple_of(i * rows, rows), rows)
 
-    def z_copy(src, s, i, way):
-        to = z + 1 if way == 0 else z - 1
-        return remote(
-            src, fw.at[s, span(i)], zsend.at[way, s, i], zrecv.at[s, i], (me, to)
-        )
-
-    def own(i):
-        return x_ref.at[span(i)]
+    def half(ref, h):
+        return ref.at[:, pl.ds(h * width, width)]
 
     def held(s, i):
         return fw.at[s, span(i)]
 
-    def scatter(src, s, i, start):
-        for h in range(2):
-            dest = 2 * s + h
-            piece = src.at[:, pl.ds(h * width, width)]
-
-            @pl.when(dest == me)
+    def to_owner(src, r, i, h, send, dest):
+        return remote(half(src, h), xg.at[r, span(i)], send, xrecv.at[r, i], (dest, z))
+
+    def express(src, s, i, start):
+        @pl.when((chip == last) & (z < Z - 1))
+        def _():
+            go(remote(src, held(s, i), esend.at[s, i], zrecv.at[s, i], (me, z + 1)), start)
+
+        @pl.when((chip == 0) & (z > 0))
+        def _():
+            go(remote(src, held(s, i), esend.at[s, i], zrecv.at[s, i], (me, z - 1)), start)
+
+    def own_slab(i, start):
+        src = x_ref.at[span(i)]
+        express(src, z, i, start)
+
+        @pl.when(z == chip)
+        def _():
+            for h in range(2):
+                @pl.when(h == core)
+                def _():
+                    if start:
+                        pltpu.make_async_copy(
+                            half(src, h), xg.at[me, span(i)], xrecv.at[me, i]
+                        ).start()
+
+                @pl.when(h != core)
+                def _():
+                    go(to_owner(src, me, i, h, xsend.at[z, i, h], sibling), start)
+
+        @pl.when((z == side) | (z == above))
+        def _():
+            for h in range(2):
+                go(to_owner(src, me, i, h, xsend.at[z, i, h], 2 * z + h), start)
+
+        @pl.when(z == opposite)
+        def _():
+            go(
+                remote(src, held(z, i), xsend.at[z, i, 0], zrecv.at[z, i], (2 * via + core, z)),
+                start,
+            )
+
+    def relay(i, start):
+        @pl.when(z == other)
+        def _():
+            r = 2 * via + core
+            if start:
+                remote(held(z, i), held(z, i), rsend.at[i, 0], zrecv.at[z, i], (r, z)).wait_recv()
+            for h in range(2):
+                go(to_owner(held(z, i), r, i, h, rsend.at[i, h], 2 * z + h), start)
+
+    def ways(o):
+        return (
+            (z >= chip) & (z < Z - 1) & (o != last),
+            (z <= chip) & (z > 0) & (o != 0),
+        )
+
+    def x_arrived(r, i):
+        pltpu.make_async_copy(xg.at[r, span(i)], xg.at[r, span(i)], xrecv.at[r, i]).wait()
+
+    def line(o, i, start):
+        right, left = ways(o)
+        for k in range(2):
+            r = 2 * o + k
+            if start:
+                @pl.when(right | left)
+                def _():
+                    x_arrived(r, i)
+            for way, there in ((0, right), (1, left)):
+                @pl.when(there)
+                def _():
+                    go(
+                        remote(
+                            xg.at[r, span(i)], xg.at[r, span(i)], lsend.at[way, r, i],
+                            xrecv.at[r, i], (me, z + 1 - 2 * way),
+                        ),
+                        start,
+                    )
+
+    def express_on(t, i, start):
+        for s, there in (
+            (z - t, (chip == last) & (z - t >= 0)),
+            (z + t, (chip == 0) & (z + t < Z)),
+        ):
+            @pl.when(there)
             def _():
                 if start:
-                    pltpu.make_async_copy(piece, xg.at[me, span(i)], xrecv.at[me, i]).start()
-
-            @pl.when(dest != me)
+                    remote(held(s, i), held(s, i), esend.at[s, i], zrecv.at[s, i], (me, 0)).wait_recv()
+                express(held(s, i), s, i, start)
+                for h in range(2):
+                    go(to_owner(held(s, i), me, i, h, xsend.at[s, i, h], 2 * s + h), start)
+
+    def y_arrived(r):
+        pltpu.make_async_copy(yg.at[r], yg.at[r], yrecv.at[r]).wait()
+
+    def y_direct(n, c):
+        return remote(y_ref, yg.at[me], ysend.at[n], yrecv.at[me], (2 * c + core, z))
+
+    def y_sibling():
+        return remote(y_ref, yg.at[me], ysend.at[2], yrecv.at[me], (sibling, z))
+
+    def y_local():
+        return pltpu.make_async_copy(y_ref, yg.at[me], lsem)
+
+    def y_relay():
+        r = 2 * via + core
+        return remote(yg.at[r], yg.at[r], psend, yrecv.at[r], (2 * other + core, z))
+
+    def y_share(n):
+        r = 2 * order[n] + core
+        return remote(yg.at[r], yg.at[r], fsend.at[n - 1], yrecv.at[r], (sibling, z))
+
+    tile = 256
+    units = CHUNKS // FOLD
+
+    def product(o, u):
+        right, left = ways(o)
+        for k in range(2):
+            r = 2 * o + k
+
+            @pl.when(jnp.logical_not(right | left))
             def _():
-                copy = remote(
-                    piece, xg.at[me, span(i)], xsend.at[s, i, h], xrecv.at[me, i], (dest, z)
-                )
-                if start:
-                    copy.start()
-                else:
-                    copy.wait_send()
-
-    def move_along(start):
-        @pl.loop(0, CHUNKS)
-        def _(i):
-            for way, there in ((0, z < Z - 1), (1, z > 0)):
-                @pl.when(there)
-                def _():
-                    copy = z_copy(own(i), z, i, way)
-                    if start:
-                        copy.start()
-                    else:
-                        copy.wait_send()
-            scatter(own(i), z, i, start)
-
-        if start:
-            send_out_grads()
-
-        for t in range(1, Z):
-            @pl.loop(0, CHUNKS)
-            def _(i):
-                for way, s, exists, further in (
-                    (0, z - t, z - t >= 0, z < Z - 1),
-                    (1, z + t, z + t < Z, z > 0),
-                ):
-                    @pl.when(exists)
-                    def _():
-                        if start:
-                            z_copy(held(s, i), s, i, way).wait_recv()
-
-                        @pl.when(further)
-                        def _():
-                            copy = z_copy(held(s, i), s, i, way)
-                            if start:
-                                copy.start()
-                            else:
-                                copy.wait_send()
-                        scatter(held(s, i), s, i, start)
-
-            if start and t == Z - 2:
-                share_out_grads()
-
-    def y_copy(j):
-        return remote(
-            y_ref, yg.at[me], ysend.at[j], yrecv.at[me], (((chip + j) % chips) * 2 + core, z)
-        )
-
-    def sibling_copy():
-        return remote(y_ref, yg.at[me], ysend.at[0], yrecv.at[me], (sibling, z))
-
-    def share_copy(j):
-        r = ((chip + j) % chips) * 2 + core
-        return remote(yg.at[r], yg.at[r], fsend.at[j], yrecv.at[r], (sibling, z))
-
-    def local_y():
-        return pltpu.make_async_copy(y_ref, yg.at[me], lsem)
-
-    def send_out_grads():
-        for j in range(1, chips):
-            y_copy(j).start()
-        sibling_copy().start()
-        local_y().start()
-
-    def share_out_grads():
-        for j in range(1, chips):
-            r = ((chip + j) % chips) * 2 + core
-            remote(yg.at[r], yg.at[r], fsend.at[j], yrecv.at[r], (sibling, z)).wait_recv()
-            share_copy(j).start()
-
-    move_along(True)
-
-    local_y().wait()
-    for j in range(chips):
-        r = ((chip + j) % chips) * 2 + 1 - core
-        remote(yg.at[r], yg.at[r], fsend.at[j], yrecv.at[r], (sibling, z)).wait_recv()
-
-    tile = 256
-
-    @pl.loop(0, CHUNKS)
-    def _(i):
-        @pl.loop(0, R)
-        def _(r):
-            pltpu.make_async_copy(xg.at[r, span(i)], xg.at[r, span(i)], xrecv.at[r, i]).wait()
+                for f in range(FOLD):
+                    x_arrived(r, u * FOLD + f)
+
+            at_k = pl.ds(pl.multiple_of(u * FOLD * rows, FOLD * rows), FOLD * rows)
 
             @pl.loop(0, columns // tile)
             def _(q):
                 at = pl.ds(pl.multiple_of(q * tile, tile), tile)
-                product = lax.dot_general(
-                    xg[r, span(i), :], yg[r, span(i), at], (((0,), (0,)), ((), ())),
+                value = lax.dot_general(
+                    xg[r, at_k, :], yg[r, at_k, at], (((0,), (0,)), ((), ())),
                     preferred_element_type=jnp.float32,
                 )
 
-                @pl.when(i == 0)
+                @pl.when(u == 0)
                 def _():
-                    grads[r, :, at] = product
-
-                @pl.when(i > 0)
+                    grads[r, :, at] = value
+
+                @pl.when(u > 0)
                 def _():
-                    grads[r, :, at] += product
+                    grads[r, :, at] += value
+
+    @pl.loop(0, CHUNKS)
+    def _(i):
+        own_slab(i, True)
+
+    @pl.loop(0, CHUNKS)
+    def _(i):
+        line(order[0], i, True)
+        relay(i, True)
+        express_on(1, i, True)
+
+        @pl.when(i == CHUNKS // 4)
+        def _():
+            y_sibling().start()
+            y_direct(0, via).start()
+            y_direct(1, other).start()
+            y_local().start()
+
+    y_local().wait()
+    y_arrived(sibling)
+
+    @pl.loop(0, CHUNKS)
+    def _(i):
+        line(order[1], i, True)
+        express_on(2, i, True)
+
+        @pl.when(i >= CHUNKS - units)
+        def _():
+            product(order[0], i - (CHUNKS - units))
+
+    y_arrived(2 * via + core)
+    y_relay().start()
+    y_arrived(2 * other + core)
+    for n in (1, 2):
+        y_share(n).start()
+
+    @pl.loop(0, CHUNKS)
+    def _(i):
+        line(order[2], i, True)
+        express_on(3, i, True)
+
+        @pl.when(i == CHUNKS - units)
+        def _():
+            y_arrived(2 * side + 1 - core)
+            y_arrived(2 * above + 1 - core)
+
+        @pl.when(i >= CHUNKS - units)
+        def _():
+            product(order[1], i - (CHUNKS - units))
+
+    y_arrived(2 * opposite + core)
+    y_share(3).start()
+
+    @pl.loop(0, CHUNKS)
+    def _(i):
+        line(order[3], i, True)
+
+    @pl.loop(0, units)
+    def _(u):
+        product(order[2], u)
+
+    y_arrived(2 * opposite + 1 - core)
+
+    @pl.loop(0, units)
+    def _(u):
+        product(order[3], u)
 
     pairs = pair_list(R)
 
@@ -303,11 +406,21 @@
             total = total + weights[r] * grads[r, at, :]
         out_ref[at, :] = total
 
-    move_along(False)
-    for j in range(1, chips):
-        y_copy(j).wait_send()
-        share_copy(j).wait_send()
-    sibling_copy().wait_send()
+    @pl.loop(0, CHUNKS)
+    def _(i):
+        own_slab(i, False)
+        relay(i, False)
+        for n in range(4):
+            line(order[n], i, False)
+        for t in range(1, 4):
+            express_on(t, i, False)
+
+    y_sibling().wait_send()
+    y_direct(0, via).wait_send()
+    y_direct(1, other).wait_send()
+    y_relay().wait_send()
+    for n in (1, 2, 3):
+        y_share(n).wait_send()
     for j in range(1, Z):
         around_z(j).wait_send()
     for j in range(1, R):
@@ -338,13 +451,16 @@
             pltpu.VMEM((2, kept, 128), jnp.float32),
             pltpu.VMEM((Z - 1, kept, 128), jnp.float32),
             pltpu.VMEM((R - 1, kept, 128), jnp.float32),
-            dma((2, Z, CHUNKS)),
+            dma((Z, CHUNKS)),
             dma((Z, CHUNKS)),
             dma((Z, CHUNKS, 2)),
             dma((R, CHUNKS)),
-            dma((R // 2,)),
+            dma((CHUNKS, 2)),
+            dma((2, R, CHUNKS)),
+            dma((3,)),
             dma((R,)),
-            dma((R // 2,)),
+            dma,
+            dma((3,)),
             dma,
             dma((Z - 1,)),
             dma((Z - 1,)),
@@ -370,7 +486,7 @@
         columns = out_grads.shape[1]
         width = slab * Z // R
         fits = (
-            R == 2 * Z and R <= 8 and width % 128 == 0 and columns % 256 == 0
+            R == 8 and Z == 4 and width % 128 == 0 and columns % 256 == 0
             and tokens % (CHUNKS * 16) == 0
             and R * (2 * tokens * (width + columns) + 4 * width * columns) < 50 * 2**20
         )

time: 300 us -> 294 us (0.980)
  Pallas kernels: 296 us -> 290 us
    pallas_call x1, Pallas kernels: 296 us -> 290 us  [by_tiles(): pl.pallas_call(functools.partial(kernel, R, Z), out_shape=(jax.ShapeDtype...]
where the time goes in v2:
time: 294 us
  Pallas kernels  290 us (99%)
  local copies, waits for them, and re-layouts  3.56 us (1%)
    pallas_call x1, Pallas kernels, by_tiles(): pl.pallas_call(functools.partial(kernel, R, Z), out_shape=(jax.ShapeDtype...  290 us

profile of v2, /device:TPU:0, one launch (start us, length us, event | category | flops | bytes accessed | tf_op | source)
XLA Modules:
  0.0 293.9 jit_solution(16664745140000724875)
XLA Ops:
  0.0 290.3 %shard_map.28 = (f32[640,1024]{1,0:T(8,128)}, bf16[4,1024,1280]{2,1,0:T(8,128)(2,1)}) custom-call(bf16[1024,1280]{1,0:T(8,128)(2,1)} %x_ref.1, bf16[1024,1024]{1,0:T(8,128)(2,1)} %y_ref.1), custom_call_target="tpu_custom_call" | custom-call | flops 10737418240 | bytes 27262976 | tf_op jit(solution)/shard_map/pallas_call | solution.py:436
  290.3 3.6 %copy.4 = f32[640,1024]{1,0:T(8,128)} copy(f32[640,1024]{1,0:T(8,128)} %get-tuple-element.6) | data formatting | bytes 5242880

commit v3 on v2

--- a/solution.py
+++ b/solution.py
@@ -9,7 +9,7 @@
 epsilon = 1e-06
 MESH = pl.DeviceIdType.MESH
 CHUNKS = 8
-FOLD = 2
+FOLD = 4
 
 
 def swapped(x, axis, apart):
@@ -106,8 +106,8 @@
     last = chips - 1
     chip, core = me // 2, me % 2
     sibling = chip * 2 + 1 - core
-    rows = x_ref.shape[0] // CHUNKS
-    width = xg.shape[2]
+    width = xg.shape[1]
+    rows = width // CHUNKS
     columns = yg.shape[2]
 
     def across(c, way):
@@ -141,14 +141,11 @@
     def span(i):
         return pl.ds(pl.multiple_of(i * rows, rows), rows)
 
-    def half(ref, h):
-        return ref.at[:, pl.ds(h * width, width)]
-
     def held(s, i):
-        return fw.at[s, span(i)]
+        return fw.at[s, :, span(i)]
 
     def to_owner(src, r, i, h, send, dest):
-        return remote(half(src, h), xg.at[r, span(i)], send, xrecv.at[r, i], (dest, z))
+        return remote(src.at[h], xg.at[r, span(i)], send, xrecv.at[r, i], (dest, z))
 
     def express(src, s, i, start):
         @pl.when((chip == last) & (z < Z - 1))
@@ -160,7 +157,7 @@
             go(remote(src, held(s, i), esend.at[s, i], zrecv.at[s, i], (me, z - 1)), start)
 
     def own_slab(i, start):
-        src = x_ref.at[span(i)]
+        src = x_ref.at[:, span(i)]
         express(src, z, i, start)
 
         @pl.when(z == chip)
@@ -170,7 +167,7 @@
                 def _():
                     if start:
                         pltpu.make_async_copy(
-                            half(src, h), xg.at[me, span(i)], xrecv.at[me, i]
+                            src.at[h], xg.at[me, span(i)], xrecv.at[me, i]
                         ).start()
 
                 @pl.when(h != core)
@@ -272,23 +269,14 @@
                 for f in range(FOLD):
                     x_arrived(r, u * FOLD + f)
 
-            at_k = pl.ds(pl.multiple_of(u * FOLD * rows, FOLD * rows), FOLD * rows)
+            block = pl.ds(pl.multiple_of(u * FOLD * rows, FOLD * rows), FOLD * rows)
 
             @pl.loop(0, columns // tile)
             def _(q):
                 at = pl.ds(pl.multiple_of(q * tile, tile), tile)
-                value = lax.dot_general(
-                    xg[r, at_k, :], yg[r, at_k, at], (((0,), (0,)), ((), ())),
-                    preferred_element_type=jnp.float32,
+                grads[r, block, at] = jnp.dot(
+                    xg[r, block, :], yg[r, :, at], preferred_element_type=jnp.float32
                 )
-
-                @pl.when(u == 0)
-                def _():
-                    grads[r, :, at] = value
-
-                @pl.when(u > 0)
-                def _():
-                    grads[r, :, at] += value
 
     @pl.loop(0, CHUNKS)
     def _(i):
@@ -437,7 +425,7 @@
         functools.partial(kernel, R, Z),
         out_shape=(
             jax.ShapeDtypeStruct((width, columns), jnp.float32),
-            jax.ShapeDtypeStruct((Z, tokens, slab), jnp.bfloat16),
+            jax.ShapeDtypeStruct((Z, 2, width, tokens), jnp.bfloat16),
         ),
         in_specs=[pl.BlockSpec(memory_space=pl.ANY)] * 2,
         out_specs=(
@@ -445,7 +433,7 @@
             pl.BlockSpec(memory_space=pl.ANY),
         ),
         scratch_shapes=[
-            pltpu.VMEM((R, tokens, width), jnp.bfloat16),
+            pltpu.VMEM((R, width, tokens), jnp.bfloat16),
             pltpu.VMEM((R, tokens, columns), jnp.bfloat16),
             pltpu.VMEM((R, width, columns), jnp.float32),
             pltpu.VMEM((2, kept, 128), jnp.float32),
@@ -475,7 +463,7 @@
             bytes_accessed=2 * R * tokens * (width + columns),
             transcendentals=0,
         ),
-    )(activations, out_grads)[0]
+    )(activations.T.reshape(2, width, tokens), out_grads)[0]
 
 
 def solution(mesh):
@@ -487,7 +475,7 @@
         width = slab * Z // R
         fits = (
             R == 8 and Z == 4 and width % 128 == 0 and columns % 256 == 0
-            and tokens % (CHUNKS * 16) == 0
+            and tokens % 128 == 0 and width % (CHUNKS * 16) == 0
             and R * (2 * tokens * (width + columns) + 4 * width * columns) < 50 * 2**20
         )
         if fits:

time: 294 us -> 285 us (0.969)
  Pallas kernels: 290 us -> 277 us
  local copies, waits for them, and re-layouts: 3.56 us -> 7.94 us
    pallas_call x1, Pallas kernels: 290 us -> 277 us  [by_tiles(): pl.pallas_call(functools.partial(kernel, R, Z), out_shape=(jax.ShapeDtype...]
    transpose x0 -> x1, local copies, waits for them, and re-layouts: none -> 4.38 us  [by_tiles(): activations.T.reshape(2, width, tokens)]
where the time goes in v3:
time: 285 us
  Pallas kernels  277 us (97%)
  local copies, waits for them, and re-layouts  7.94 us (3%)
    pallas_call x1, Pallas kernels, by_tiles(): pl.pallas_call(functools.partial(kernel, R, Z), out_shape=(jax.ShapeDtype...  277 us

profile of v3, /device:TPU:0, one launch (start us, length us, event | category | flops | bytes accessed | tf_op | source)
XLA Modules:
  0.0 284.9 jit_solution(10883116267773669128)
XLA Ops:
  0.0 4.4 %copy.3 = bf16[1280,1024]{1,0:T(8,128)(2,1)} copy(bf16[1280,1024]{0,1:T(8,128)(2,1)} %bitcast.2) | data formatting | bytes 5242880 | tf_op jit(solution)/shard_map/transpose | solution.py:466
  4.4 277.0 %shard_map.28 = (f32[640,1024]{1,0:T(8,128)}, bf16[4,2,640,1024]{3,2,1,0:T(8,128)(2,1)}) custom-call(bf16[2,640,1024]{2,1,0:T(8,128)(2,1)} %bitcast.3, bf16[1024,1024]{1,0:T(8,128)(2,1)} %y_ref.1), custom_call_target="tpu_custom_call" | custom-call | flops 10737418240 | bytes 27262976 | tf_op jit(solution)/shard_map/pallas_call | solution.py:424
  281.4 3.6 %copy.5 = f32[640,1024]{1,0:T(8,128)} copy(f32[640,1024]{1,0:T(8,128)} %get-tuple-element.6) | data formatting | bytes 5242880

commit v4 on v3

--- a/solution.py
+++ b/solution.py
@@ -8,8 +8,8 @@
 
 epsilon = 1e-06
 MESH = pl.DeviceIdType.MESH
-CHUNKS = 8
-FOLD = 4
+CHUNKS = 20
+FOLD = 10
 
 
 def swapped(x, axis, apart):
@@ -223,6 +223,16 @@
                         start,
                     )
 
+    def pace(n, i):
+        @pl.when((z == chip) & (i > 0))
+        def _():
+            line(order[n], i - 1, False)
+
+        if n > 0:
+            @pl.when((z == chip) & (i == 0))
+            def _():
+                line(order[n - 1], CHUNKS - 1, False)
+
     def express_on(t, i, start):
         for s, there in (
             (z - t, (chip == last) & (z - t >= 0)),
@@ -281,14 +291,12 @@
     @pl.loop(0, CHUNKS)
     def _(i):
         own_slab(i, True)
-
-    @pl.loop(0, CHUNKS)
-    def _(i):
         line(order[0], i, True)
+        pace(0, i)
         relay(i, True)
         express_on(1, i, True)
 
-        @pl.when(i == CHUNKS // 4)
+        @pl.when(i == CHUNKS // 2)
         def _():
             y_sibling().start()
             y_direct(0, via).start()
@@ -301,6 +309,7 @@
     @pl.loop(0, CHUNKS)
     def _(i):
         line(order[1], i, True)
+        pace(1, i)
         express_on(2, i, True)
 
         @pl.when(i >= CHUNKS - units)
@@ -316,6 +325,7 @@
     @pl.loop(0, CHUNKS)
     def _(i):
         line(order[2], i, True)
+        pace(2, i)
         express_on(3, i, True)
 
         @pl.when(i == CHUNKS - units)
@@ -333,6 +343,7 @@
     @pl.loop(0, CHUNKS)
     def _(i):
         line(order[3], i, True)
+        pace(3, i)
 
     @pl.loop(0, units)
     def _(u):
@@ -398,8 +409,16 @@
     def _(i):
         own_slab(i, False)
         relay(i, False)
-        for n in range(4):
-            line(order[n], i, False)
+
+        @pl.when(z != chip)
+        def _():
+            for n in range(4):
+                line(order[n], i, False)
+
+        @pl.when((z == chip) & (i == CHUNKS - 1))
+        def _():
+            line(order[3], i, False)
+
         for t in range(1, 4):
             express_on(t, i, False)
 

time: 285 us -> 364 us (1.28)
  Pallas kernels: 277 us -> 355 us
    pallas_call x1, Pallas kernels: 277 us -> 355 us  [by_tiles(): pl.pallas_call(functools.partial(kernel, R, Z), out_shape=(jax.ShapeDtype...]
where the time goes in v4:
time: 364 us; the launch traced here: 363 us
  Pallas kernels  355 us (98%)
  local copies, waits for them, and re-layouts  7.94 us (2%)
    pallas_call x1, Pallas kernels, by_tiles(): pl.pallas_call(functools.partial(kernel, R, Z), out_shape=(jax.ShapeDtype...  355 us

profile of v4, /device:TPU:0, one launch (start us, length us, event | category | flops | bytes accessed | tf_op | source)
XLA Modules:
  0.0 363.1 jit_solution(7133937378562162072)
XLA Ops:
  0.0 4.4 %copy.3 = bf16[1280,1024]{1,0:T(8,128)(2,1)} copy(bf16[1280,1024]{0,1:T(8,128)(2,1)} %bitcast.2) | data formatting | bytes 5242880 | tf_op jit(solution)/shard_map/transpose | solution.py:485
  4.4 355.1 %shard_map.28 = (f32[640,1024]{1,0:T(8,128)}, bf16[4,2,640,1024]{3,2,1,0:T(8,128)(2,1)}) custom-call(bf16[2,640,1024]{2,1,0:T(8,128)(2,1)} %bitcast.3, bf16[1024,1024]{1,0:T(8,128)(2,1)} %y_ref.1), custom_call_target="tpu_custom_call" | custom-call | flops 10737418240 | bytes 27262976 | tf_op jit(solution)/shard_map/pallas_call | solution.py:443
  359.5 3.6 copy.5

commit v5 on v3

--- a/solution.py
+++ b/solution.py
@@ -9,7 +9,6 @@
 epsilon = 1e-06
 MESH = pl.DeviceIdType.MESH
 CHUNKS = 8
-FOLD = 4
 
 
 def swapped(x, axis, apart):
@@ -94,11 +93,25 @@
     return [w for _, w in sorted(weights[0], key=lambda item: item[0])]
 
 
-def kernel(
-    R, Z, x_ref, y_ref, out_ref, fw,
-    xg, yg, grads, part, first, second,
+def meet(R, Z, me, z):
+    barrier = pltpu.get_barrier_semaphore()
+    for j in range(1, Z):
+        pl.semaphore_signal(barrier, inc=1, device_id=(me, (z + j) % Z), device_id_type=MESH)
+    for j in range(1, R):
+        pl.semaphore_signal(barrier, inc=1, device_id=((me + j) % R, z), device_id_type=MESH)
+    pl.semaphore_wait(barrier, Z + R - 2)
+
+
+def remote(src, dst, send, recv, device):
+    return pltpu.make_async_remote_copy(
+        src_ref=src, dst_ref=dst, send_sem=send, recv_sem=recv,
+        device_id=device, device_id_type=MESH,
+    )
+
+
+def gather_kernel(
+    R, Z, x_ref, y_ref, xg, yg, fw,
     esend, zrecv, xsend, xrecv, rsend, lsend, ysend, yrecv, psend, fsend, lsem,
-    asend, arecv, bsend, brecv,
 ):
     me = lax.axis_index("dp")
     z = lax.axis_index("tensor")
@@ -108,7 +121,6 @@
     sibling = chip * 2 + 1 - core
     width = xg.shape[1]
     rows = width // CHUNKS
-    columns = yg.shape[2]
 
     def across(c, way):
         return (c // 2) * 2 + 1 - c % 2 if way == 0 else (1 - c // 2) * 2 + c % 2
@@ -119,18 +131,7 @@
     via = jnp.where(core == 0, side, above)
     other = jnp.where(core == 0, above, side)
 
-    barrier = pltpu.get_barrier_semaphore()
-    for j in range(1, Z):
-        pl.semaphore_signal(barrier, inc=1, device_id=(me, (z + j) % Z), device_id_type=MESH)
-    for j in range(1, R):
-        pl.semaphore_signal(barrier, inc=1, device_id=((me + j) % R, z), device_id_type=MESH)
-    pl.semaphore_wait(barrier, Z + R - 2)
-
-    def remote(src, dst, send, recv, device):
-        return pltpu.make_async_remote_copy(
-            src_ref=src, dst_ref=dst, send_sem=send, recv_sem=recv,
-            device_id=device, device_id_type=MESH,
-        )
+    meet(R, Z, me, z)
 
     def go(copy, start):
         if start:
@@ -256,28 +257,6 @@
         r = 2 * order[n] + core
         return remote(yg.at[r], yg.at[r], fsend.at[n - 1], yrecv.at[r], (sibling, z))
 
-    tile = 256
-    units = CHUNKS // FOLD
-
-    def product(o, u):
-        right, left = ways(o)
-        for k in range(2):
-            r = 2 * o + k
-
-            @pl.when(jnp.logical_not(right | left))
-            def _():
-                for f in range(FOLD):
-                    x_arrived(r, u * FOLD + f)
-
-            block = pl.ds(pl.multiple_of(u * FOLD * rows, FOLD * rows), FOLD * rows)
-
-            @pl.loop(0, columns // tile)
-            def _(q):
-                at = pl.ds(pl.multiple_of(q * tile, tile), tile)
-                grads[r, block, at] = jnp.dot(
-                    xg[r, block, :], yg[r, :, at], preferred_element_type=jnp.float32
-                )
-
     @pl.loop(0, CHUNKS)
     def _(i):
         own_slab(i, True)
@@ -302,10 +281,6 @@
     def _(i):
         line(order[1], i, True)
         express_on(2, i, True)
-
-        @pl.when(i >= CHUNKS - units)
-        def _():
-            product(order[0], i - (CHUNKS - units))
 
     y_arrived(2 * via + core)
     y_relay().start()
@@ -318,15 +293,6 @@
         line(order[2], i, True)
         express_on(3, i, True)
 
-        @pl.when(i == CHUNKS - units)
-        def _():
-            y_arrived(2 * side + 1 - core)
-            y_arrived(2 * above + 1 - core)
-
-        @pl.when(i >= CHUNKS - units)
-        def _():
-            product(order[1], i - (CHUNKS - units))
-
     y_arrived(2 * opposite + core)
     y_share(3).start()
 
@@ -334,15 +300,65 @@
     def _(i):
         line(order[3], i, True)
 
-    @pl.loop(0, units)
-    def _(u):
-        product(order[2], u)
-
-    y_arrived(2 * opposite + 1 - core)
-
-    @pl.loop(0, units)
-    def _(u):
-        product(order[3], u)
+    for o in (side, above, opposite):
+        y_arrived(2 * o + 1 - core)
+
+    @pl.loop(0, CHUNKS)
+    def _(i):
+        for o in order:
+            right, left = ways(o)
+            for k in range(2):
+                @pl.when(jnp.logical_not(right | left))
+                def _():
+                    x_arrived(2 * o + k, i)
+
+    @pl.loop(0, CHUNKS)
+    def _(i):
+        own_slab(i, False)
+        relay(i, False)
+        for n in range(4):
+            line(order[n], i, False)
+        for t in range(1, 4):
+            express_on(t, i, False)
+
+    y_sibling().wait_send()
+    y_direct(0, via).wait_send()
+    y_direct(1, other).wait_send()
+    y_relay().wait_send()
+    for n in (1, 2, 3):
+        y_share(n).wait_send()
+
+def combine_kernel(
+    R, Z, x_ref, y_ref, out_ref,
+    xg, yg, grads, part, first, second, xsem, ysem, asend, arecv, bsend, brecv,
+):
+    me = lax.axis_index("dp")
+    z = lax.axis_index("tensor")
+    width, columns = out_ref.shape
+    tile = 256
+    copies = [
+        (
+            pltpu.make_async_copy(x_ref.at[r], xg.at[r], xsem.at[r]),
+            pltpu.make_async_copy(y_ref.at[r], yg.at[r], ysem.at[r]),
+        )
+        for r in range(R)
+    ]
+    for x_copy, y_copy in copies:
+        x_copy.start()
+        y_copy.start()
+
+    meet(R, Z, me, z)
+
+    for r in range(R):
+        for copy in copies[r]:
+            copy.wait()
+
+        @pl.loop(0, columns // tile)
+        def _(q):
+            at = pl.ds(pl.multiple_of(q * tile, tile), tile)
+            grads[r, :, at] = jnp.dot(
+                xg[r], yg[r, :, at], preferred_element_type=jnp.float32
+            )
 
     pairs = pair_list(R)
 
@@ -394,21 +410,6 @@
             total = total + weights[r] * grads[r, at, :]
         out_ref[at, :] = total
 
-    @pl.loop(0, CHUNKS)
-    def _(i):
-        own_slab(i, False)
-        relay(i, False)
-        for n in range(4):
-            line(order[n], i, False)
-        for t in range(1, 4):
-            express_on(t, i, False)
-
-    y_sibling().wait_send()
-    y_direct(0, via).wait_send()
-    y_direct(1, other).wait_send()
-    y_relay().wait_send()
-    for n in (1, 2, 3):
-        y_share(n).wait_send()
     for j in range(1, Z):
         around_z(j).wait_send()
     for j in range(1, R):
@@ -421,24 +422,17 @@
     width = slab * Z // R
     kept = -(-len(pair_list(R)) // 8) * 8
     dma = pltpu.SemaphoreType.DMA
-    return pl.pallas_call(
-        functools.partial(kernel, R, Z),
+    anywhere = pl.BlockSpec(memory_space=pl.ANY)
+    x_all, y_all, _ = pl.pallas_call(
+        functools.partial(gather_kernel, R, Z),
         out_shape=(
-            jax.ShapeDtypeStruct((width, columns), jnp.float32),
+            jax.ShapeDtypeStruct((R, width, tokens), jnp.bfloat16),
+            jax.ShapeDtypeStruct((R, tokens, columns), jnp.bfloat16),
             jax.ShapeDtypeStruct((Z, 2, width, tokens), jnp.bfloat16),
         ),
-        in_specs=[pl.BlockSpec(memory_space=pl.ANY)] * 2,
-        out_specs=(
-            pl.BlockSpec(memory_space=pltpu.VMEM),
-            pl.BlockSpec(memory_space=pl.ANY),
-        ),
+        in_specs=[anywhere] * 2,
+        out_specs=(anywhere,) * 3,
         scratch_shapes=[
-            pltpu.VMEM((R, width, tokens), jnp.bfloat16),
-            pltpu.VMEM((R, tokens, columns), jnp.bfloat16),
-            pltpu.VMEM((R, width, columns), jnp.float32),
-            pltpu.VMEM((2, kept, 128), jnp.float32),
-            pltpu.VMEM((Z - 1, kept, 128), jnp.float32),
-            pltpu.VMEM((R - 1, kept, 128), jnp.float32),
             dma((Z, CHUNKS)),
             dma((Z, CHUNKS)),
             dma((Z, CHUNKS, 2)),
@@ -450,20 +444,36 @@
             dma,
             dma((3,)),
             dma,
+        ],
+        compiler_params=pltpu.CompilerParams(
+            collective_id=0, has_side_effects=True, vmem_limit_bytes=60 * 1024 * 1024
+        ),
+        name="gather_inputs",
+    )(activations.T.reshape(2, width, tokens), out_grads)
+    return pl.pallas_call(
+        functools.partial(combine_kernel, R, Z),
+        out_shape=jax.ShapeDtypeStruct((width, columns), jnp.float32),
+        in_specs=[anywhere] * 2,
+        out_specs=pl.BlockSpec(memory_space=pltpu.VMEM),
+        scratch_shapes=[
+            pltpu.VMEM((R, width, tokens), jnp.bfloat16),
+            pltpu.VMEM((R, tokens, columns), jnp.bfloat16),
+            pltpu.VMEM((R, width, columns), jnp.float32),
+            pltpu.VMEM((2, kept, 128), jnp.float32),
+            pltpu.VMEM((Z - 1, kept, 128), jnp.float32),
+            pltpu.VMEM((R - 1, kept, 128), jnp.float32),
+            dma((R,)),
+            dma((R,)),
             dma((Z - 1,)),
             dma((Z - 1,)),
             dma((R - 1,)),
             dma((R - 1,)),
         ],
         compiler_params=pltpu.CompilerParams(
-            collective_id=0, has_side_effects=True, vmem_limit_bytes=60 * 1024 * 1024
+            collective_id=1, has_side_effects=True, vmem_limit_bytes=60 * 1024 * 1024
         ),
-        cost_estimate=pl.CostEstimate(
-            flops=2 * R * tokens * width * columns,
-            bytes_accessed=2 * R * tokens * (width + columns),
-            transcendentals=0,
-        ),
-    )(activations.T.reshape(2, width, tokens), out_grads)[0]
+        name="combine",
+    )(x_all, y_all)
 
 
 def solution(mesh):

time: 285 us -> 312 us (1.095)
  Pallas kernels: 277 us -> 303 us
    pallas_call x1 -> x2, Pallas kernels: 277 us -> 303 us  [the longest x1 225 us: by_tiles(): pl.pallas_call(functools.partial(gather_kernel, R, Z), out_shape=(jax.Sha...]
where the time goes in v5:
time: 312 us; the launch traced here: 311 us
  Pallas kernels  303 us (97%)
  local copies, waits for them, and re-layouts  7.94 us (3%)
    pallas_call x1, Pallas kernels, by_tiles(): pl.pallas_call(functools.partial(gather_kernel, R, Z), out_shape=(jax.Sha...  225 us
    pallas_call x1, Pallas kernels, by_tiles(): pl.pallas_call(functools.partial(combine_kernel, R, Z), out_shape=jax.Sha...  78.2 us

profile of v5, /device:TPU:0, one launch (start us, length us, event | category | flops | bytes accessed | tf_op | source)
XLA Modules:
  0.0 311.4 jit_solution(3648683186850360297)
XLA Ops:
  0.0 4.4 %copy.3 = bf16[1280,1024]{1,0:T(8,128)(2,1)} copy(bf16[1280,1024]{0,1:T(8,128)(2,1)} %bitcast.3) | data formatting | bytes 5242880 | tf_op jit(solution)/shard_map/transpose | solution.py:452
  4.4 225.2 %gather_inputs.1 = (bf16[8,640,1024]{2,1,0:T(8,128)(2,1)}, bf16[8,1024,1024]{2,1,0:T(8,128)(2,1)}, bf16[4,2,640,1024]{3,2,1,0:T(8,128)(2,1)}) custom-call(bf16[2,640,1024]{2,1,0:T(8,128)(2,1)} %bitcast.2, bf16[1024,1024]{1,0:T(8,128)(2,1)} %y_ref.1), custom_call_target="tpu_custom_call" | custom-call | tf_op jit(solution)/shard_map/gather_inputs/pallas_call | solution.py:426
  229.6 78.2 %combine.1 = f32[640,1024]{1,0:T(8,128)} custom-call(bf16[8,640,1024]{2,1,0:T(8,128)(2,1)} %get-tuple-element.7.x_ref, bf16[8,1024,1024]{2,1,0:T(8,128)(2,1)} %get-tuple-element.8.y_ref), custom_call_target="tpu_custom_call" | custom-call | tf_op jit(solution)/shard_map/combine/pallas_call | solution.py:453
  307.8 3.6 %copy.5 = f32[640,1024]{1,0:T(8,128)} copy(f32[640,1024]{1,0:T(8,128)} %combine.1) | data formatting | bytes 5242880

commit v6 on v3

--- a/solution.py
+++ b/solution.py
@@ -8,8 +8,8 @@
 
 epsilon = 1e-06
 MESH = pl.DeviceIdType.MESH
-CHUNKS = 8
-FOLD = 4
+CHUNKS = 10
+FOLD = 5
 
 
 def swapped(x, axis, apart):
@@ -97,7 +97,7 @@
 def kernel(
     R, Z, x_ref, y_ref, out_ref, fw,
     xg, yg, grads, part, first, second,
-    esend, zrecv, xsend, xrecv, rsend, lsend, ysend, yrecv, psend, fsend, lsem,
+    esend, zrecv, xsend, xrecv, rsend, lsend, ysend, yrecv, fsend, lsem,
     asend, arecv, bsend, brecv,
 ):
     me = lax.axis_index("dp")
@@ -158,7 +158,6 @@
 
     def own_slab(i, start):
         src = x_ref.at[:, span(i)]
-        express(src, z, i, start)
 
         @pl.when(z == chip)
         def _():
@@ -223,6 +222,18 @@
                         start,
                     )
 
+    def pace(members, i):
+        @pl.when((z == chip) & (i > 0))
+        def _():
+            for o in members:
+                line(o, i - 1, False)
+
+    def drain(members):
+        @pl.when(z == chip)
+        def _():
+            for o in members:
+                line(o, CHUNKS - 1, False)
+
     def express_on(t, i, start):
         for s, there in (
             (z - t, (chip == last) & (z - t >= 0)),
@@ -239,18 +250,16 @@
     def y_arrived(r):
         pltpu.make_async_copy(yg.at[r], yg.at[r], yrecv.at[r]).wait()
 
-    def y_direct(n, c):
-        return remote(y_ref, yg.at[me], ysend.at[n], yrecv.at[me], (2 * c + core, z))
+    def y_direct(n):
+        return remote(
+            y_ref, yg.at[me], ysend.at[n], yrecv.at[me], (2 * order[n] + core, z)
+        )
 
     def y_sibling():
-        return remote(y_ref, yg.at[me], ysend.at[2], yrecv.at[me], (sibling, z))
+        return remote(y_ref, yg.at[me], ysend.at[0], yrecv.at[me], (sibling, z))
 
     def y_local():
         return pltpu.make_async_copy(y_ref, yg.at[me], lsem)
-
-    def y_relay():
-        r = 2 * via + core
-        return remote(yg.at[r], yg.at[r], psend, yrecv.at[r], (2 * other + core, z))
 
     def y_share(n):
         r = 2 * order[n] + core
@@ -284,65 +293,68 @@
 
     @pl.loop(0, CHUNKS)
     def _(i):
-        line(order[0], i, True)
-        relay(i, True)
+        express(x_ref.at[:, span(i)], z, i, True)
+        line(chip, i, True)
         express_on(1, i, True)
-
-        @pl.when(i == CHUNKS // 4)
-        def _():
-            y_sibling().start()
-            y_direct(0, via).start()
-            y_direct(1, other).start()
-            y_local().start()
-
-    y_local().wait()
-    y_arrived(sibling)
+        pace((chip,), i)
+
+        @pl.when(i >= CHUNKS // 2)
+        def _():
+            relay(2 * i - CHUNKS, True)
+            relay(2 * i - CHUNKS + 1, True)
+
+    y_sibling().start()
+    y_local().start()
+    for n in (1, 2, 3):
+        y_direct(n).start()
 
     @pl.loop(0, CHUNKS)
     def _(i):
-        line(order[1], i, True)
-        express_on(2, i, True)
+        line(side, i, True)
+        line(above, i, True)
+
+        @pl.when(i == 0)
+        def _():
+            drain((chip,))
+
+        for f in range(2):
+            m = 2 * i + f
+            for t in range(2, Z):
+                @pl.when(m // CHUNKS == t - 2)
+                def _():
+                    express_on(t, m % CHUNKS, True)
+
+        pace((side, above), i)
+
+        @pl.when(i == CHUNKS - units)
+        def _():
+            y_local().wait()
+            y_arrived(sibling)
 
         @pl.when(i >= CHUNKS - units)
         def _():
-            product(order[0], i - (CHUNKS - units))
-
-    y_arrived(2 * via + core)
-    y_relay().start()
-    y_arrived(2 * other + core)
-    for n in (1, 2):
-        y_share(n).start()
+            product(chip, i - (CHUNKS - units))
 
     @pl.loop(0, CHUNKS)
     def _(i):
-        line(order[2], i, True)
-        express_on(3, i, True)
-
-        @pl.when(i == CHUNKS - units)
-        def _():
-            y_arrived(2 * side + 1 - core)
-            y_arrived(2 * above + 1 - core)
-
-        @pl.when(i >= CHUNKS - units)
-        def _():
-            product(order[1], i - (CHUNKS - units))
-
-    y_arrived(2 * opposite + core)
-    y_share(3).start()
-
-    @pl.loop(0, CHUNKS)
-    def _(i):
-        line(order[3], i, True)
-
-    @pl.loop(0, units)
-    def _(u):
-        product(order[2], u)
-
-    y_arrived(2 * opposite + 1 - core)
-
-    @pl.loop(0, units)
-    def _(u):
-        product(order[3], u)
+        line(opposite, i, True)
+
+        @pl.when(i == 0)
+        def _():
+            drain((side, above))
+
+        pace((opposite,), i)
+
+    for n in (1, 2, 3):
+        y_arrived(2 * order[n] + core)
+        y_share(n).start()
+
+    for n in (1, 2, 3):
+        y_arrived(2 * order[n] + 1 - core)
+
+        @pl.loop(0, units)
+        def _(u):
+            product(order[n], u)
 
     pairs = pair_list(R)
 
@@ -397,17 +409,20 @@
     @pl.loop(0, CHUNKS)
     def _(i):
         own_slab(i, False)
+        express(x_ref.at[:, span(i)], z, i, False)
         relay(i, False)
-        for n in range(4):
-            line(order[n], i, False)
-        for t in range(1, 4):
+        for t in range(1, Z):
             express_on(t, i, False)
 
+        @pl.when(z != chip)
+        def _():
+            for o in order:
+                line(o, i, False)
+
+    drain((opposite,))
     y_sibling().wait_send()
-    y_direct(0, via).wait_send()
-    y_direct(1, other).wait_send()
-    y_relay().wait_send()
     for n in (1, 2, 3):
+        y_direct(n).wait_send()
         y_share(n).wait_send()
     for j in range(1, Z):
         around_z(j).wait_send()
@@ -445,9 +460,8 @@
             dma((R, CHUNKS)),
             dma((CHUNKS, 2)),
             dma((2, R, CHUNKS)),
-            dma((3,)),
+            dma((4,)),
             dma((R,)),
-            dma,
             dma((3,)),
             dma,
             dma((Z - 1,)),

time: 285 us -> 306 us (1.074)
  Pallas kernels: 277 us -> 298 us
    pallas_call x1, Pallas kernels: 277 us -> 298 us  [by_tiles(): pl.pallas_call(functools.partial(kernel, R, Z), out_shape=(jax.ShapeDtype...]
where the time goes in v6:
time: 306 us; the launch traced here: 305 us
  Pallas kernels  298 us (97%)
  local copies, waits for them, and re-layouts  7.94 us (3%)
    pallas_call x1, Pallas kernels, by_tiles(): pl.pallas_call(functools.partial(kernel, R, Z), out_shape=(jax.ShapeDtype...  298 us

profile of v6, /device:TPU:0, one launch (start us, length us, event | category | flops | bytes accessed | tf_op | source)
XLA Modules:
  0.0 305.5 jit_solution(17123683346202643922)
XLA Ops:
  0.0 4.4 %copy.3 = bf16[1280,1024]{1,0:T(8,128)(2,1)} copy(bf16[1280,1024]{0,1:T(8,128)(2,1)} %bitcast.2) | data formatting | bytes 5242880 | tf_op jit(solution)/shard_map/transpose | solution.py:480
  4.4 297.5 %shard_map.28 = (f32[640,1024]{1,0:T(8,128)}, bf16[4,2,640,1024]{3,2,1,0:T(8,128)(2,1)}) custom-call(bf16[2,640,1024]{2,1,0:T(8,128)(2,1)} %bitcast.3, bf16[1024,1024]{1,0:T(8,128)(2,1)} %y_ref.1), custom_call_target="tpu_custom_call" | custom-call | flops 10737418240 | bytes 27262976 | tf_op jit(solution)/shard_map/pallas_call | solution.py:439
  301.9 3.6 %copy.5 = f32[640,1024]{1,0:T(8,128)} copy(f32[640,1024]{1,0:T(8,128)} %get-tuple-element.6) | data formatting | bytes 5242880

commit v7 on v1

--- a/solution.py
+++ b/solution.py
@@ -8,7 +8,8 @@
 
 epsilon = 1e-06
 MESH = pl.DeviceIdType.MESH
-CHUNKS = 4
+CHUNKS = 8
+FOLD = 4
 
 
 def swapped(x, axis, apart):
@@ -103,8 +104,8 @@
     chips = R // 2
     chip, core = me // 2, me % 2
     sibling = chip * 2 + 1 - core
-    rows = x_ref.shape[0] // CHUNKS
-    width = xg.shape[2]
+    width = xg.shape[1]
+    rows = width // CHUNKS
     columns = yg.shape[2]
 
     barrier = pltpu.get_barrier_semaphore()
@@ -126,19 +127,19 @@
     def z_copy(src, s, i, way):
         to = z + 1 if way == 0 else z - 1
         return remote(
-            src, fw.at[s, span(i)], zsend.at[way, s, i], zrecv.at[s, i], (me, to)
+            src, fw.at[s, :, span(i)], zsend.at[way, s, i], zrecv.at[s, i], (me, to)
         )
 
     def own(i):
-        return x_ref.at[span(i)]
+        return x_ref.at[:, span(i)]
 
     def held(s, i):
-        return fw.at[s, span(i)]
+        return fw.at[s, :, span(i)]
 
     def scatter(src, s, i, start):
         for h in range(2):
             dest = 2 * s + h
-            piece = src.at[:, pl.ds(h * width, width)]
+            piece = src.at[h]
 
             @pl.when(dest == me)
             def _():
@@ -192,8 +193,6 @@
                                 copy.wait_send()
                         scatter(held(s, i), s, i, start)
 
-            if start and t == Z - 2:
-                share_out_grads()
 
     def y_copy(j):
         return remote(
@@ -223,6 +222,7 @@
             share_copy(j).start()
 
     move_along(True)
+    share_out_grads()
 
     local_y().wait()
     for j in range(chips):
@@ -231,27 +231,22 @@
 
     tile = 256
 
-    @pl.loop(0, CHUNKS)
-    def _(i):
+    @pl.loop(0, CHUNKS // FOLD)
+    def _(u):
         @pl.loop(0, R)
         def _(r):
-            pltpu.make_async_copy(xg.at[r, span(i)], xg.at[r, span(i)], xrecv.at[r, i]).wait()
+            for f in range(FOLD):
+                i = u * FOLD + f
+                pltpu.make_async_copy(xg.at[r, span(i)], xg.at[r, span(i)], xrecv.at[r, i]).wait()
+
+            block = pl.ds(pl.multiple_of(u * FOLD * rows, FOLD * rows), FOLD * rows)
 
             @pl.loop(0, columns // tile)
             def _(q):
                 at = pl.ds(pl.multiple_of(q * tile, tile), tile)
-                product = lax.dot_general(
-                    xg[r, span(i), :], yg[r, span(i), at], (((0,), (0,)), ((), ())),
-                    preferred_element_type=jnp.float32,
+                grads[r, block, at] = jnp.dot(
+                    xg[r, block, :], yg[r, :, at], preferred_element_type=jnp.float32
                 )
-
-                @pl.when(i == 0)
-                def _():
-                    grads[r, :, at] = product
-
-                @pl.when(i > 0)
-                def _():
-                    grads[r, :, at] += product
 
     pairs = pair_list(R)
 
@@ -324,7 +319,7 @@
         functools.partial(kernel, R, Z),
         out_shape=(
             jax.ShapeDtypeStruct((width, columns), jnp.float32),
-            jax.ShapeDtypeStruct((Z, tokens, slab), jnp.bfloat16),
+            jax.ShapeDtypeStruct((Z, 2, width, tokens), jnp.bfloat16),
         ),
         in_specs=[pl.BlockSpec(memory_space=pl.ANY)] * 2,
         out_specs=(
@@ -332,7 +327,7 @@
             pl.BlockSpec(memory_space=pl.ANY),
         ),
         scratch_shapes=[
-            pltpu.VMEM((R, tokens, width), jnp.bfloat16),
+            pltpu.VMEM((R, width, tokens), jnp.bfloat16),
             pltpu.VMEM((R, tokens, columns), jnp.bfloat16),
             pltpu.VMEM((R, width, columns), jnp.float32),
             pltpu.VMEM((2, kept, 128), jnp.float32),
@@ -359,7 +354,7 @@
             bytes_accessed=2 * R * tokens * (width + columns),
             transcendentals=0,
         ),
-    )(activations, out_grads)[0]
+    )(activations.T.reshape(2, width, tokens), out_grads)[0]
 
 
 def solution(mesh):
@@ -370,8 +365,8 @@
         columns = out_grads.shape[1]
         width = slab * Z // R
         fits = (
-            R == 2 * Z and R <= 8 and width % 128 == 0 and columns % 256 == 0
-            and tokens % (CHUNKS * 16) == 0
+            R == 8 and Z == 4 and width % 128 == 0 and columns % 256 == 0
+            and tokens % 128 == 0 and width % (CHUNKS * 16) == 0
             and R * (2 * tokens * (width + columns) + 4 * width * columns) < 50 * 2**20
         )
         if fits:

time: 300 us -> 274 us (0.913)
  Pallas kernels: 296 us -> 265 us
  local copies, waits for them, and re-layouts: 3.56 us -> 7.94 us
    pallas_call x1, Pallas kernels: 296 us -> 265 us  [by_tiles(): pl.pallas_call(functools.partial(kernel, R, Z), out_shape=(jax.ShapeDtype...]
    transpose x0 -> x1, local copies, waits for them, and re-layouts: none -> 4.38 us  [by_tiles(): activations.T.reshape(2, width, tokens)]
where the time goes in v7:
time: 274 us; the launch traced here: 273 us
  Pallas kernels  265 us (97%)
  local copies, waits for them, and re-layouts  7.94 us (3%)
    pallas_call x1, Pallas kernels, by_tiles(): pl.pallas_call(functools.partial(kernel, R, Z), out_shape=(jax.ShapeDtype...  265 us

profile of v7, /device:TPU:0, one launch (start us, length us, event | category | flops | bytes accessed | tf_op | source)
XLA Modules:
  0.0 273.0 jit_solution(15591134764243196876)
XLA Ops:
  0.0 4.4 %copy.3 = bf16[1280,1024]{1,0:T(8,128)(2,1)} copy(bf16[1280,1024]{0,1:T(8,128)(2,1)} %bitcast.2) | data formatting | bytes 5242880 | tf_op jit(solution)/shard_map/transpose | solution.py:357
  4.4 265.0 %shard_map.28 = (f32[640,1024]{1,0:T(8,128)}, bf16[4,2,640,1024]{3,2,1,0:T(8,128)(2,1)}) custom-call(bf16[2,640,1024]{2,1,0:T(8,128)(2,1)} %bitcast.3, bf16[1024,1024]{1,0:T(8,128)(2,1)} %y_ref.1), custom_call_target="tpu_custom_call" | custom-call | flops 10737418240 | bytes 27262976 | tf_op jit(solution)/shard_map/pallas_call | solution.py:318
  269.4 3.6 %copy.5 = f32[640,1024]{1,0:T(8,128)} copy(f32[640,1024]{1,0:T(8,128)} %get-tuple-element.6) | data formatting | bytes 5242880

commit v8 on v7

--- a/solution.py
+++ b/solution.py
@@ -10,6 +10,7 @@
 MESH = pl.DeviceIdType.MESH
 CHUNKS = 8
 FOLD = 4
+LAG = 2
 
 
 def swapped(x, axis, apart):
@@ -95,9 +96,10 @@
 
 
 def kernel(
-    R, Z, x_ref, y_ref, out_ref, fw,
+    R, Z, x_ref, y_ref, out_ref, fw, held_over,
     xg, yg, grads, part, first, second,
-    zsend, zrecv, xsend, xrecv, ysend, yrecv, fsend, lsem, asend, arecv, bsend, brecv,
+    zsend, zrecv, xsend, xrecv, ysend, yrecv, fsend, lsem, rrecv, rsend,
+    asend, arecv, bsend, brecv,
 ):
     me = lax.axis_index("dp")
     z = lax.axis_index("tensor")
@@ -106,6 +108,14 @@
     sibling = chip * 2 + 1 - core
     width = xg.shape[1]
     rows = width // CHUNKS
+
+    def across(c, way):
+        return (c // 2) * 2 + 1 - c % 2 if way == 0 else (1 - c // 2) * 2 + c % 2
+
+    side, above = across(chip, 0), across(chip, 1)
+    opposite = across(side, 1)
+    via = jnp.where(core == 0, side, above)
+    other = jnp.where(core == 0, above, side)
     columns = yg.shape[2]
 
     barrier = pltpu.get_barrier_semaphore()
@@ -136,25 +146,62 @@
     def held(s, i):
         return fw.at[s, :, span(i)]
 
+    def go(copy, start):
+        if start:
+            copy.start()
+        else:
+            copy.wait_send()
+
     def scatter(src, s, i, start):
+        @pl.when(s == opposite)
+        def _():
+            go(
+                remote(
+                    src, held_over.at[:, span(i)], xsend.at[s, i, 0], rrecv.at[i],
+                    (2 * via + core, z),
+                ),
+                start,
+            )
+
+        @pl.when(s != opposite)
+        def _():
+            for h in range(2):
+                dest = 2 * s + h
+                piece = src.at[h]
+
+                @pl.when(dest == me)
+                def _():
+                    if start:
+                        pltpu.make_async_copy(piece, xg.at[me, span(i)], xrecv.at[me, i]).start()
+
+                @pl.when(dest != me)
+                def _():
+                    go(
+                        remote(
+                            piece, xg.at[me, span(i)], xsend.at[s, i, h], xrecv.at[me, i],
+                            (dest, z),
+                        ),
+                        start,
+                    )
+
+    def relay(i, start):
+        r = 2 * via + core
+        here = held_over.at[:, span(i)]
+        if start:
+            remote(here, here, rsend.at[i, 0], rrecv.at[i], (r, z)).wait_recv()
         for h in range(2):
-            dest = 2 * s + h
-            piece = src.at[h]
-
-            @pl.when(dest == me)
-            def _():
-                if start:
-                    pltpu.make_async_copy(piece, xg.at[me, span(i)], xrecv.at[me, i]).start()
-
-            @pl.when(dest != me)
-            def _():
-                copy = remote(
-                    piece, xg.at[me, span(i)], xsend.at[s, i, h], xrecv.at[me, i], (dest, z)
-                )
-                if start:
-                    copy.start()
-                else:
-                    copy.wait_send()
+            go(
+                remote(
+                    held_over.at[h, span(i)], xg.at[r, span(i)], rsend.at[i, h], xrecv.at[r, i],
+                    (2 * other + h, z),
+                ),
+                start,
+            )
+
+    def relay_after(t, i):
+        @pl.when((z - other == t) | (other - z == t))
+        def _():
+            relay(i, True)
 
     def move_along(start):
         @pl.loop(0, CHUNKS)
@@ -193,6 +240,17 @@
                                 copy.wait_send()
                         scatter(held(s, i), s, i, start)
 
+                if start:
+                    relay_after(t - 1, i)
+                if start and t == Z - 1:
+                    @pl.when(i >= LAG)
+                    def _():
+                        relay_after(t, i - LAG)
+
+                    @pl.when(i == CHUNKS // 2)
+                    def _():
+                        share_out_grads()
+
 
     def y_copy(j):
         return remote(
@@ -222,7 +280,8 @@
             share_copy(j).start()
 
     move_along(True)
-    share_out_grads()
+    for f in range(LAG):
+        relay_after(Z - 1, CHUNKS - LAG + f)
 
     local_y().wait()
     for j in range(chips):
@@ -230,23 +289,6 @@
         remote(yg.at[r], yg.at[r], fsend.at[j], yrecv.at[r], (sibling, z)).wait_recv()
 
     tile = 256
-
-    @pl.loop(0, CHUNKS // FOLD)
-    def _(u):
-        @pl.loop(0, R)
-        def _(r):
-            for f in range(FOLD):
-                i = u * FOLD + f
-                pltpu.make_async_copy(xg.at[r, span(i)], xg.at[r, span(i)], xrecv.at[r, i]).wait()
-
-            block = pl.ds(pl.multiple_of(u * FOLD * rows, FOLD * rows), FOLD * rows)
-
-            @pl.loop(0, columns // tile)
-            def _(q):
-                at = pl.ds(pl.multiple_of(q * tile, tile), tile)
-                grads[r, block, at] = jnp.dot(
-                    xg[r, block, :], yg[r, :, at], preferred_element_type=jnp.float32
-                )
 
     pairs = pair_list(R)
 
@@ -259,9 +301,27 @@
                 sums[n] = sums[n] + blocks[a] * blocks[c]
         return tuple(sums)
 
-    sums = lax.fori_loop(
-        0, width // 8, accumulate, tuple(jnp.zeros((8, 128), jnp.float32) for _ in pairs)
-    )
+    def products(u):
+        @pl.loop(0, R)
+        def _(r):
+            for f in range(FOLD):
+                i = u * FOLD + f
+                pltpu.make_async_copy(xg.at[r, span(i)], xg.at[r, span(i)], xrecv.at[r, i]).wait()
+
+            block = pl.ds(u * FOLD * rows, FOLD * rows)
+
+            @pl.loop(0, columns // tile)
+            def _(q):
+                at = pl.ds(pl.multiple_of(q * tile, tile), tile)
+                grads[r, block, at] = jnp.dot(
+                    xg[r, block, :], yg[r, :, at], preferred_element_type=jnp.float32
+                )
+
+    sums = tuple(jnp.zeros((8, 128), jnp.float32) for _ in pairs)
+    bands = FOLD * rows // 8
+    for u in range(CHUNKS // FOLD):
+        products(u)
+        sums = lax.fori_loop(u * bands, (u + 1) * bands, accumulate, sums)
     part[0] = jnp.zeros(part.shape[1:], jnp.float32)
     for n in range(len(pairs)):
         part[0, pl.ds(n, 1), :] = jnp.sum(sums[n], axis=0, keepdims=True)
@@ -299,6 +359,11 @@
         out_ref[at, :] = total
 
     move_along(False)
+
+    @pl.loop(0, CHUNKS)
+    def _(i):
+        relay(i, False)
+
     for j in range(1, chips):
         y_copy(j).wait_send()
         share_copy(j).wait_send()
@@ -320,10 +385,12 @@
         out_shape=(
             jax.ShapeDtypeStruct((width, columns), jnp.float32),
             jax.ShapeDtypeStruct((Z, 2, width, tokens), jnp.bfloat16),
+            jax.ShapeDtypeStruct((2, width, tokens), jnp.bfloat16),
         ),
         in_specs=[pl.BlockSpec(memory_space=pl.ANY)] * 2,
         out_specs=(
             pl.BlockSpec(memory_space=pltpu.VMEM),
+            pl.BlockSpec(memory_space=pl.ANY),
             pl.BlockSpec(memory_space=pl.ANY),
         ),
         scratch_shapes=[
@@ -341,6 +408,8 @@
             dma((R,)),
             dma((R // 2,)),
             dma,
+            dma((CHUNKS,)),
+            dma((CHUNKS, 2)),
             dma((Z - 1,)),
             dma((Z - 1,)),
             dma((R - 1,)),

time: 274 us -> 297 us (1.084)
  Pallas kernels: 265 us -> 288 us
    pallas_call x1, Pallas kernels: 265 us -> 288 us  [by_tiles(): pl.pallas_call(functools.partial(kernel, R, Z), out_shape=(jax.ShapeDtype...]
where the time goes in v8:
time: 297 us; the launch traced here: 296 us
  Pallas kernels  288 us (97%)
  local copies, waits for them, and re-layouts  7.94 us (3%)
    pallas_call x1, Pallas kernels, by_tiles(): pl.pallas_call(functools.partial(kernel, R, Z), out_shape=(jax.ShapeDtype...  288 us

profile of v8, /device:TPU:0, one launch (start us, length us, event | category | flops | bytes accessed | tf_op | source)
XLA Modules:
  0.0 296.0 jit_solution(10901353915995785676)
XLA Ops:
  0.0 4.4 %copy.3 = bf16[1280,1024]{1,0:T(8,128)(2,1)} copy(bf16[1280,1024]{0,1:T(8,128)(2,1)} %bitcast.2) | data formatting | bytes 5242880 | tf_op jit(solution)/shard_map/transpose | solution.py:426
  4.4 288.0 %shard_map.28 = (f32[640,1024]{1,0:T(8,128)}, bf16[4,2,640,1024]{3,2,1,0:T(8,128)(2,1)}, bf16[2,640,1024]{2,1,0:T(8,128)(2,1)}) custom-call(bf16[2,640,1024]{2,1,0:T(8,128)(2,1)} %bitcast.3, bf16[1024,1024]{1,0:T(8,128)(2,1)} %y_ref.1), custom_call_target="tpu_custom_call" | custom-call | flops 10737418240 | bytes 27262976 | tf_op jit(solution)/shard_map/pallas_call | solution.py:383
  292.4 3.6 %copy.5 = f32[640,1024]{1,0:T(8,128)} copy(f32[640,1024]{1,0:T(8,128)} %get-tuple-element.6) | data formatting | bytes 5242880

commit v9 on v7

--- a/solution.py
+++ b/solution.py
@@ -10,6 +10,7 @@
 MESH = pl.DeviceIdType.MESH
 CHUNKS = 8
 FOLD = 4
+WINDOW = 3
 
 
 def swapped(x, axis, apart):
@@ -162,11 +163,16 @@
             for way, there in ((0, z < Z - 1), (1, z > 0)):
                 @pl.when(there)
                 def _():
-                    copy = z_copy(own(i), z, i, way)
                     if start:
-                        copy.start()
+                        z_copy(own(i), z, i, way).start()
+
+                        @pl.when(i >= WINDOW)
+                        def _():
+                            z_copy(own(i - WINDOW), z, i - WINDOW, way).wait_send()
                     else:
-                        copy.wait_send()
+                        @pl.when(i >= CHUNKS - WINDOW)
+                        def _():
+                            z_copy(own(i), z, i, way).wait_send()
             scatter(own(i), z, i, start)
 
         if start:

time: 274 us -> 285 us (1.040)
  Pallas kernels: 265 us -> 277 us
    pallas_call x1, Pallas kernels: 265 us -> 277 us  [by_tiles(): pl.pallas_call(functools.partial(kernel, R, Z), out_shape=(jax.ShapeDtype...]
where the time goes in v9:
time: 285 us
  Pallas kernels  277 us (97%)
  local copies, waits for them, and re-layouts  7.94 us (3%)
    pallas_call x1, Pallas kernels, by_tiles(): pl.pallas_call(functools.partial(kernel, R, Z), out_shape=(jax.ShapeDtype...  277 us

profile of v9, /device:TPU:0, one launch (start us, length us, event | category | flops | bytes accessed | tf_op | source)
XLA Modules:
  0.0 284.8 jit_solution(15404653982026776335)
XLA Ops:
  0.0 4.4 %copy.3 = bf16[1280,1024]{1,0:T(8,128)(2,1)} copy(bf16[1280,1024]{0,1:T(8,128)(2,1)} %bitcast.2) | data formatting | bytes 5242880 | tf_op jit(solution)/shard_map/transpose | solution.py:363
  4.4 276.8 %shard_map.28 = (f32[640,1024]{1,0:T(8,128)}, bf16[4,2,640,1024]{3,2,1,0:T(8,128)(2,1)}) custom-call(bf16[2,640,1024]{2,1,0:T(8,128)(2,1)} %bitcast.3, bf16[1024,1024]{1,0:T(8,128)(2,1)} %y_ref.1), custom_call_target="tpu_custom_call" | custom-call | flops 10737418240 | bytes 27262976 | tf_op jit(solution)/shard_map/pallas_call | solution.py:324
  281.2 3.6 %copy.5 = f32[640,1024]{1,0:T(8,128)} copy(f32[640,1024]{1,0:T(8,128)} %get-tuple-element.6) | data formatting | bytes 5242880

commit v10 on v7

--- a/solution.py
+++ b/solution.py
@@ -8,8 +8,8 @@
 
 epsilon = 1e-06
 MESH = pl.DeviceIdType.MESH
-CHUNKS = 8
-FOLD = 4
+CHUNKS = 4
+FOLD = 2
 
 
 def swapped(x, axis, apart):

time: 274 us -> 279 us (1.018)
  Pallas kernels: 265 us -> 271 us
    pallas_call x1, Pallas kernels: 265 us -> 271 us  [by_tiles(): pl.pallas_call(functools.partial(kernel, R, Z), out_shape=(jax.ShapeDtype...]
where the time goes in v10:
time: 279 us
  Pallas kernels  271 us (97%)
  local copies, waits for them, and re-layouts  7.94 us (3%)
    pallas_call x1, Pallas kernels, by_tiles(): pl.pallas_call(functools.partial(kernel, R, Z), out_shape=(jax.ShapeDtype...  271 us

profile of v10, /device:TPU:0, one launch (start us, length us, event | category | flops | bytes accessed | tf_op | source)
XLA Modules:
  0.0 278.6 jit_solution(17627895355413106906)
XLA Ops:
  0.0 4.4 %copy.3 = bf16[1280,1024]{1,0:T(8,128)(2,1)} copy(bf16[1280,1024]{0,1:T(8,128)(2,1)} %bitcast.2) | data formatting | bytes 5242880 | tf_op jit(solution)/shard_map/transpose | solution.py:357
  4.4 270.6 %shard_map.28 = (f32[640,1024]{1,0:T(8,128)}, bf16[4,2,640,1024]{3,2,1,0:T(8,128)(2,1)}) custom-call(bf16[2,640,1024]{2,1,0:T(8,128)(2,1)} %bitcast.3, bf16[1024,1024]{1,0:T(8,128)(2,1)} %y_ref.1), custom_call_target="tpu_custom_call" | custom-call | flops 10737418240 | bytes 27262976 | tf_op jit(solution)/shard_map/pallas_call | solution.py:318
  275.0 3.6 %copy.5 = f32[640,1024]{1,0:T(8,128)} copy(f32[640,1024]{1,0:T(8,128)} %get-tuple-element.6) | data formatting | bytes 5242880
